TPU v7x, 32 devices: a whole 2x2x4 slice. The times are simulated.
32 devices in a mesh: dp: 8 (over z, core), expert: 4 (over y, x).
Axes of the slice: x: 2, y: 2, z: 4, core: 2. Of those that a mesh axis runs over, the one named last changes fastest.
Arguments:
- tokens: bfloat16 [4, 1024, 3584], P('expert', 'dp'), may hold values from -6 to 6
- grad_out: bfloat16 [4, 1024, 3584], P('expert', 'dp'), may hold values from -6 to 6
- route_ids: int32 [4, 1024], P('expert', 'dp'), may hold values from 0 to 3, as said below
- route_gates: float32 [4, 1024], P('expert', 'dp'), may hold values from 0.2 to 1
- w_gate: bfloat16 [4, 3584, 1024], P('expert', 'dp'), may hold values from -0.09375 to 0.09375
- w_up: bfloat16 [4, 3584, 1024], P('expert', 'dp'), may hold values from -0.09375 to 0.09375
- w_down: bfloat16 [4, 1024, 3584], P('expert', 'dp'), may hold values from -0.1875 to 0.1875
Outputs:
- moe_out: bfloat16 [4, 1024, 3584], P('expert', 'dp')
- input_grad: bfloat16 [4, 1024, 3584], P('expert', None, 'dp')
- gate_grad: float32 [4, 1024], P('expert', 'dp')
Inputs may be any that keep to these rules, and one draw needn't show every extreme that they name: `route_ids`: among the 128 tokens of one device at most 80 name the same expert; one expert is named by exactly 80 tokens of every device; on one device the counts of the other experts differ by at most one.
All inputs are finite; a program needn't handle non-finite values.
Results may differ from a plain program's by a relative error of at most 0.0057.
Values may be sent and summed in bfloat16 or wider, within the bound.
A program may use at most 128 MiB of HBM per device.

v0:
```python
import jax
import jax.numpy as jnp
from jax import lax
from jax.sharding import PartitionSpec as P


def slot_table(route_line, expert_count, capacity):
    chosen = (route_line[:, None] == jnp.arange(expert_count, dtype=jnp.int32)[None, :]).astype(
        jnp.int32
    )
    placed = jnp.sum((jnp.cumsum(chosen, axis=0) - 1) * chosen, axis=1)
    return route_line * capacity + placed


def local(tokens, grad_out, route_ids, route_gates, w_gate, w_up, w_down):
    expert_count = lax.axis_size("expert")
    tok_count = tokens.shape[1]
    width = tokens.shape[2]
    capacity = max(2, 5 * tok_count // (2 * expert_count))
    own_ids = route_ids[0]
    own_slots = slot_table(own_ids, expert_count, capacity)
    slot_owner = jnp.full((expert_count * capacity,), tok_count, jnp.int32)
    slot_owner = slot_owner.at[own_slots].set(jnp.arange(tok_count, dtype=jnp.int32))
    own_tokens = tokens[0]
    own_grad = grad_out[0]
    gate_column = route_gates[0][:, None]
    scaled_grad = (gate_column * own_grad.astype(jnp.float32)).astype(jnp.bfloat16)
    zero_row = jnp.zeros((1, width), jnp.bfloat16)
    send_tokens = jnp.concatenate([own_tokens, zero_row])[slot_owner].reshape(
        expert_count, capacity, width
    )
    send_grad = jnp.concatenate([scaled_grad, zero_row])[slot_owner].reshape(
        expert_count, capacity, width
    )
    arrived_tokens = lax.all_to_all(send_tokens, "expert", split_axis=0, concat_axis=0, tiled=True)
    routed = arrived_tokens.reshape(expert_count * capacity, width)
    full_gate, full_up, full_down = (
        lax.all_gather(w_gate, "dp", axis=1, tiled=True),
        lax.all_gather(w_up, "dp", axis=1, tiled=True),
        lax.all_gather(w_down, "dp", axis=1, tiled=True),
    )
    gate_matrix = full_gate[0]
    up_matrix = full_up[0]
    down_matrix = full_down[0]
    gate_pre = jnp.dot(routed, gate_matrix, preferred_element_type=jnp.float32)
    up_pre = jnp.dot(routed, up_matrix, preferred_element_type=jnp.float32)
    sigmoid_gate = jax.nn.sigmoid(gate_pre)
    silu_gate = gate_pre * sigmoid_gate
    hidden = (silu_gate * up_pre).astype(jnp.bfloat16)
    expert_out = jnp.dot(hidden, down_matrix, preferred_element_type=jnp.float32).astype(
        jnp.bfloat16
    )
    returned = lax.all_to_all(
        expert_out.reshape(expert_count, capacity, width),
        "expert",
        split_axis=0,
        concat_axis=0,
        tiled=True,
    )
    token_out = returned.reshape(expert_count * capacity, width)[own_slots]
    moe_out = (gate_column * token_out.astype(jnp.float32)).astype(jnp.bfloat16)
    gate_grad = jnp.sum(own_grad.astype(jnp.float32) * token_out.astype(jnp.float32), axis=1)
    arrived_grad = lax.all_to_all(send_grad, "expert", split_axis=0, concat_axis=0, tiled=True)
    routed_grad = arrived_grad.reshape(expert_count * capacity, width)
    hidden_grad = jnp.dot(routed_grad, down_matrix.T, preferred_element_type=jnp.float32)
    gate_pre_grad = (
        hidden_grad * up_pre * sigmoid_gate * (1.0 + gate_pre * (1.0 - sigmoid_gate))
    ).astype(jnp.bfloat16)
    up_pre_grad = (hidden_grad * silu_gate).astype(jnp.bfloat16)
    total = jnp.dot(gate_pre_grad, gate_matrix.T, preferred_element_type=jnp.float32)
    input_rows = (
        total + jnp.dot(up_pre_grad, up_matrix.T, preferred_element_type=jnp.float32)
    ).astype(jnp.bfloat16)
    home_rows = lax.all_to_all(
        input_rows.reshape(expert_count, capacity, width),
        "expert",
        split_axis=0,
        concat_axis=0,
        tiled=True,
    )
    token_grad = home_rows.reshape(expert_count * capacity, width)[own_slots]
    input_grad = lax.all_to_all(token_grad[None], "dp", split_axis=2, concat_axis=1, tiled=True)
    return (moe_out[None], input_grad, gate_grad[None])


def solution(mesh):
    in_specs = (
        P("expert", "dp", None),
        P("expert", "dp", None),
        P("expert", "dp"),
        P("expert", "dp"),
        P("expert", "dp", None),
        P("expert", "dp", None),
        P("expert", "dp", None),
    )
    out_specs = (P("expert", "dp", None), P("expert", None, "dp"), P("expert", "dp"))
    return jax.shard_map(local, mesh=mesh, in_specs=in_specs, out_specs=out_specs, check_vma=False)
```

profile of v0, /device:TPU:0, one launch (start us, length us, event | category | flops | bytes accessed | tf_op | source)
XLA Modules:
  0.0 416.3 jit_solution(1568874448295475949)
XLA Ops:
  11.0 3.1 gather_fusion
  14.1 32.7 %all_to_all.38 = bf16[4,80,3584]{2,1,0:T(8,128)(2,1)} all-to-all(bf16[4,80,3584]{2,1,0:T(8,128)(2,1)S(1)} %bitcast.67), channel_id=1, replica_groups=mesh['dp'=8,'expert'=4] {'expert'}, dimensions={0} | all-to-all | bytes 4587520 | tf_op jit(solution)/shard_map/all_to_all | solution.py:35
  46.8 39.0 %all-gather.4.cloned.1.call-done = bf16[1,3584,1024]{2,1,0:T(8,128)(2,1)} async-done(((bf16[1,448,1024]{2,1,0:T(8,128)(2,1)}), bf16[1,3584,1024]{2,1,0:T(8,128)(2,1)}) %all-gather.4.cloned.1.call-update) | async-done | bytes 7340048 | tf_op jit(solution)/shard_map/all_gather | solution.py:38
  85.8 7.5 %fusion.10 = f32[320,1024]{1,0:T(8,128)} fusion(bf16[320,3584]{1,0:T(8,128)(2,1)} %bitcast.72, bf16[1,3584,1024]{2,1,0:T(8,128)(2,1)} %all-gather.4.cloned.1.call-done), kind=kOutput, calls=%fused_computation.15 | convolution fusion | flops 2348810240 | bytes 10944512 | tf_op jit(solution)/shard_map/dot_general | solution.py:45
  93.3 66.2 %all-gather.6.cloned.1.call-done = bf16[1,3584,1024]{2,1,0:T(8,128)(2,1)} async-done(((bf16[1,448,1024]{2,1,0:T(8,128)(2,1)}), bf16[1,3584,1024]{2,1,0:T(8,128)(2,1)}) %all-gather.6.cloned.1.call-update) | async-done | bytes 7340048 | tf_op jit(solution)/shard_map/all_gather | solution.py:39
  159.5 6.8 %fusion.6 = f32[320,1024]{1,0:T(8,128)} fusion(bf16[320,3584]{1,0:T(8,128)(2,1)S(1)} %bitcast.73, bf16[1,3584,1024]{2,1,0:T(8,128)(2,1)} %all-gather.6.cloned.1.call-done), kind=kOutput, calls=%fused_computation.11 | convolution fusion | flops 2348810240 | bytes 10944512 | tf_op jit(solution)/shard_map/dot_general | solution.py:46
  166.2 66.9 %all-gather.8.cloned.1.call-done = bf16[1,1024,3584]{2,1,0:T(8,128)(2,1)} async-done(((bf16[1,128,3584]{2,1,0:T(8,128)(2,1)}), bf16[1,1024,3584]{2,1,0:T(8,128)(2,1)}) %all-gather.8.cloned.1.call-update) | async-done | bytes 7340048 | tf_op jit(solution)/shard_map/all_gather | solution.py:40
  233.1 7.9 %fusion.18 = bf16[320,3584]{1,0:T(8,128)(2,1)} fusion(bf16[1,1024,3584]{2,1,0:T(8,128)(2,1)} %all-gather.8.cloned.1.call-done, f32[320,1024]{1,0:T(8,128)} %fusion.6, f32[320,1024]{1,0:T(8,128)} %fusion.10), kind=kOutput, calls=%fused_computation.19 | convolution fusion | flops 2351923200 | bytes 12255232 | tf_op jit(solution)/shard_map/dot_general | solution.py:50
  241.0 3.7 all-to-all-start.1
  244.7 27.6 %all-to-all-done.1 = bf16[4,80,3584]{2,1,0:T(8,128)(2,1)S(1)} async-done(((bf16[4,80,3584]{2,1,0:T(8,128)(2,1)}), bf16[4,80,3584]{2,1,0:T(8,128)(2,1)S(1)}, u32[]{:S(2)}, u32[]{:S(2)}) %all-to-all-start.1) | async-done | bytes 2293792 | tf_op jit(solution)/shard_map/all_to_all | solution.py:53
  273.4 2.5 fusion.24
  276.0 3.1 gather_fusion.2
  279.1 30.1 %all_to_all.39 = bf16[4,80,3584]{2,1,0:T(8,128)(2,1)S(1)} all-to-all(bf16[4,80,3584]{2,1,0:T(8,128)(2,1)S(1)} %bitcast.66), channel_id=1, replica_groups=mesh['dp'=8,'expert'=4] {'expert'}, dimensions={0} | all-to-all | bytes 4587520 | tf_op jit(solution)/shard_map/all_to_all | solution.py:63
  309.3 5.8 %fusion = f32[320,1024]{1,0:T(8,128)S(1)} fusion(bf16[320,3584]{1,0:T(8,128)(2,1)S(1)} %bitcast.76, bf16[1,1024,3584]{2,1,0:T(8,128)(2,1)} %all-gather.8.cloned.1.call-done), kind=kOutput, calls=%fused_computation.5 | convolution fusion | flops 2348810240 | bytes 10944512 | tf_op jit(solution)/shard_map/dot_general | solution.py:65
  316.2 4.8 %fusion.4 = f32[320,3584]{1,0:T(8,128)} fusion(bf16[1,3584,1024]{2,1,0:T(8,128)(2,1)S(1)} %bitcast.87, f32[320,1024]{1,0:T(8,128)S(1)} %fusion, f32[320,1024]{1,0:T(8,128)S(1)} %copy-done.6), kind=kOutput, calls=%fused_computation.9 | convolution fusion | flops 2350776320 | bytes 14548992 | tf_op jit(solution)/shard_map/dot_general | solution.py:72
  320.9 6.0 %fusion.15 = bf16[320,3584]{1,0:T(8,128)(2,1)S(1)} fusion(f32[320,3584]{1,0:T(8,128)} %fusion.4, bf16[1,3584,1024]{2,1,0:T(8,128)(2,1)S(1)} %bitcast.85, f32[320,1024]{1,0:T(8,128)S(1)} %copy-done.6, f32[320,1024]{1,0:T(8,128)} %copy-done.7, f32[320,1024]{1,0:T(8,128)} %fusion.6), kind=kOutput, calls=%fused_computation.18 | convolution fusion | flops 2354380800 | bytes 18153472 | tf_op jit(solution)/shard_map/dot_general | solution.py:70
  326.9 28.4 %all_to_all.40 = bf16[4,80,3584]{2,1,0:T(8,128)(2,1)S(1)} all-to-all(bf16[4,80,3584]{2,1,0:T(8,128)(2,1)S(1)} %bitcast.75), channel_id=1, replica_groups=mesh['dp'=8,'expert'=4] {'expert'}, dimensions={0} | all-to-all | bytes 4587520 | tf_op jit(solution)/shard_map/all_to_all | solution.py:74
  356.5 2.5 copy.14
  359.5 19.7 %reduce = bf16[3584,128]{1,0:T(8,128)(2,1)S(1)} reduce(bf16[3584,1,128]{2,1,0:T(2,128)(2,1)S(1)} %bitcast.68, bf16[]{:T(256)} %broadcast.103), dimensions={1}, to_apply=%bitcast.58.reduce_sub_computation | reduce | bytes 1835010
  379.2 1.1 reshape.155
  380.3 3.6 all-to-all-start.4
  383.9 1.1 fusion.22
  385.0 22.6 %all-to-all-done.4 = bf16[8,2,28672]{2,1,0:T(2,128)(2,1)S(1)} async-done(((bf16[8,2,28672]{2,1,0:T(2,128)(2,1)}), bf16[8,2,28672]{2,1,0:T(2,128)(2,1)S(1)}, u32[]{:S(2)}, u32[]{:S(2)}) %all-to-all-start.4) | async-done | bytes 917536 | tf_op jit(solution)/shard_map/all_to_all | solution.py:82
  408.6 1.2 copy.19
  (48 shorter events, 8.6 us)
Async XLA Ops:
  7.2 2.2 copy-start.4
  7.2 2.5 copy-start.3
  7.2 78.6 %all-gather.4.cloned.1.call-start = ((), (), s32[]{:S(2)}) async-start(), calls=%async_computation.5 | async-start | bytes 8257536 | tf_op jit(solution)/shard_map/all_gather | solution.py:38
  7.9 151.5 %all-gather.6.cloned.1.call-start = ((), (), s32[]{:S(2)}) async-start(), calls=%async_computation.6 | async-start | bytes 8257536 | tf_op jit(solution)/shard_map/all_gather | solution.py:39
  8.7 224.5 %all-gather.8.cloned.1.call-start = ((), (), s32[]{:S(2)}) async-start(), calls=%async_computation.7 | async-start | bytes 8257536 | tf_op jit(solution)/shard_map/all_gather | solution.py:40
  85.8 73.7 %copy-start.2 = (bf16[4,80,3584]{2,1,0:T(8,128)(2,1)S(1)}, bf16[4,80,3584]{2,1,0:T(8,128)(2,1)}, u32[]{:S(2)}) copy-start(bf16[4,80,3584]{2,1,0:T(8,128)(2,1)} %all_to_all.38) | copy-start | bytes 6881284
  241.0 31.3 %all-to-all-start.1 = ((bf16[4,80,3584]{2,1,0:T(8,128)(2,1)}), bf16[4,80,3584]{2,1,0:T(8,128)(2,1)S(1)}, u32[]{:S(2)}, u32[]{:S(2)}) async-start(bf16[4,80,3584]{2,1,0:T(8,128)(2,1)} %bitcast.74), calls=%async_computation.1 | async-start | bytes 4587520 | tf_op jit(solution)/shard_map/all_to_all | solution.py:53
  272.3 1.1 copy-start.5
  273.4 2.5 copy-start
  279.1 37.1 %slice-start.2 = ((s8[7340032]{0:T(1024)(128)(4,1)}), s8[4194304]{0:T(1024)(128)(4,1)S(1)}, s32[]{:S(2)}) async-start(s8[7340032]{0:T(1024)(128)(4,1)} %bitcast.86), calls=%async_computation.10 | async-start | bytes 8388608
  309.3 6.9 %slice-start.3 = ((s8[7340032]{0:T(1024)(128)(4,1)}), s8[3145728]{0:T(1024)(128)(4,1)S(1)}, s32[]{:S(2)}) async-start(s8[7340032]{0:T(1024)(128)(4,1)} %bitcast.86), calls=%async_computation.11 | async-start | bytes 6291456
  309.3 6.9 %copy-start.6 = (f32[320,1024]{1,0:T(8,128)S(1)}, f32[320,1024]{1,0:T(8,128)}, u32[]{:S(2)}) copy-start(f32[320,1024]{1,0:T(8,128)} %fusion.10) | copy-start | bytes 3932164
  309.3 11.7 %slice-start = ((s8[7340032]{0:T(1024)(128)(4,1)}), s8[4194304]{0:T(1024)(128)(4,1)S(1)}, s32[]{:S(2)}) async-start(s8[7340032]{0:T(1024)(128)(4,1)} %bitcast.84), calls=%async_computation.8 | async-start | bytes 8388608
  315.1 1.1 copy-start.7
  316.2 4.8 %slice-start.1 = ((s8[7340032]{0:T(1024)(128)(4,1)}), s8[3145728]{0:T(1024)(128)(4,1)S(1)}, s32[]{:S(2)}) async-start(s8[7340032]{0:T(1024)(128)(4,1)} %bitcast.84), calls=%async_computation.9 | async-start | bytes 6291456
  379.2 4.7 %copy-start.1 = (bf16[128,3584]{1,0:T(8,128)(2,1)S(1)}, bf16[128,3584]{1,0:T(8,128)(2,1)}, u32[]{:S(2)}) copy-start(bf16[128,3584]{1,0:T(8,128)(2,1)} %copy-done) | copy-start | bytes 2752516
  380.3 27.3 %all-to-all-start.4 = ((bf16[8,2,28672]{2,1,0:T(2,128)(2,1)}), bf16[8,2,28672]{2,1,0:T(2,128)(2,1)S(1)}, u32[]{:S(2)}, u32[]{:S(2)}) async-start(bf16[8,2,28672]{2,1,0:T(2,128)(2,1)} %reshape.155), calls=%async_computation.4 | async-start | bytes 1835008 | tf_op jit(solution)/shard_map/all_to_all | solution.py:82
Sparse Core Ops, SparseCore 0:
  9.7 76.0 all-gather.3
  87.4 71.9 all-gather.5
  161.1 71.9 all-gather.7
where the time goes:
time: 417 us; the launch traced here: 416 us
  waiting for transfers between devices  224 us (54%)
  blocking collectives  91.3 us (22%)
  matrix products  38.7 us (9%)
  other arithmetic  23.7 us (6%)
  local copies, waits for them, and re-layouts  17.1 us (4%)
  between operations  14 us (3%)
  starting transfers between devices  7.35 us (2%)
    all_gather x1, waiting for transfers between devices, local(): lax.all_gather(w_down, 'dp', axis=1, tiled=True)  66.9 us
    all_gather x1, waiting for transfers between devices, local(): lax.all_gather(w_up, 'dp', axis=1, tiled=True)  66.2 us
    all_gather x1, waiting for transfers between devices, local(): lax.all_gather(w_gate, 'dp', axis=1, tiled=True)  39 us
    all_to_all x1, blocking collectives, local(): lax.all_to_all(send_tokens, 'expert', split_axis=0, concat_axis=0, tiled=...  32.7 us
    all_to_all x1, blocking collectives, local(): lax.all_to_all(send_grad, 'expert', split_axis=0, concat_axis=0, tiled=True)  30.1 us
    all_to_all x1, blocking collectives, local(): lax.all_to_all(input_rows.reshape(expert_count, capacity, width), 'expert...  28.4 us
    all_to_all x1, waiting for transfers between devices, local(): lax.all_to_all(expert_out.reshape(expert_count, capacity, width), 'expert...  27.6 us
    all_to_all x1, waiting for transfers between devices, local(): lax.all_to_all(token_grad[None], 'dp', split_axis=2, concat_axis=1, tiled...  22.6 us
  transfers between devices with their start and end apart: 5, of which 5 were waited for; matrix products, arithmetic and copies ran while one was open for 5% of the time, Pallas kernels for 0%

commit v1 on v0

v1 whole, which is shorter than its diff:
```python
import jax
import jax.numpy as jnp
from jax import lax
from jax.sharding import PartitionSpec as P

F32 = jnp.float32
BF16 = jnp.bfloat16
DOWN_PARTS = 2


def placement(route_line, expert_count, capacity):
    tok_count = route_line.shape[0]
    same = route_line[:, None] == route_line[None, :]
    earlier = jnp.arange(tok_count)[None, :] < jnp.arange(tok_count)[:, None]
    placed = jnp.sum((same & earlier).astype(jnp.int32), axis=1)
    slots = route_line * capacity + placed
    rows = jnp.arange(expert_count * capacity, dtype=jnp.int32)
    return (rows[:, None] == slots[None, :]).astype(BF16)


def mm(a, b, dims=(((1,), (0,)), ((), ()))):
    return lax.dot_general(a, b, dims, preferred_element_type=F32)


NT = (((1,), (1,)), ((), ()))
TN = (((0,), (0,)), ((), ()))


def local(tokens, grad_out, route_ids, route_gates, w_gate, w_up, w_down):
    expert_count = lax.axis_size("expert")
    dp_count = lax.axis_size("dp")
    tok_count = tokens.shape[1]
    width = tokens.shape[2]
    capacity = max(2, 5 * tok_count // (2 * expert_count))
    place = placement(route_ids[0], expert_count, capacity)
    own_grad = grad_out[0].astype(F32)
    gate_column = route_gates[0][:, None]
    scaled_grad = (gate_column * own_grad).astype(BF16)

    def over_experts(rows):
        cols = rows.shape[1]
        got = lax.all_to_all(
            rows.reshape(expert_count, capacity, cols),
            "expert", split_axis=0, concat_axis=0, tiled=True,
        )
        return got.reshape(expert_count * capacity, cols)

    gate_matrix = lax.all_gather(w_gate, "dp", axis=1, tiled=True)[0]
    up_matrix = lax.all_gather(w_up, "dp", axis=1, tiled=True)[0]
    w_down, _ = lax.optimization_barrier((w_down, gate_matrix[:16, :128]))
    step = width // DOWN_PARTS
    spans = [slice(i * step, (i + 1) * step) for i in range(DOWN_PARTS)]
    downs = [lax.all_gather(w_down[:, :, s], "dp", axis=1, tiled=True)[0] for s in spans]

    routed = over_experts(mm(place, tokens[0]).astype(BF16))
    routed_grad = over_experts(mm(place, scaled_grad).astype(BF16))

    gate_pre = mm(routed, gate_matrix)
    up_pre = mm(routed, up_matrix)
    sigmoid_gate = jax.nn.sigmoid(gate_pre)
    silu_gate = gate_pre * sigmoid_gate
    hidden = (silu_gate * up_pre).astype(BF16)

    moe_parts = []
    gate_grad = jnp.zeros((tok_count,), F32)
    hidden_grad = jnp.zeros_like(gate_pre)
    for s, down in zip(spans, downs):
        expert_out = mm(hidden, down).astype(BF16)
        hidden_grad = hidden_grad + mm(routed_grad[:, s], down, NT)
        token_out = mm(place, over_experts(expert_out), TN)
        moe_parts.append((gate_column * token_out).astype(BF16))
        gate_grad = gate_grad + jnp.sum(own_grad[:, s] * token_out, axis=1)
    moe_out = jnp.concatenate(moe_parts, axis=1)

    gate_pre_grad = (
        hidden_grad * up_pre * sigmoid_gate * (1.0 + gate_pre * (1.0 - sigmoid_gate))
    ).astype(BF16)
    up_pre_grad = (hidden_grad * silu_gate).astype(BF16)
    input_rows = (mm(gate_pre_grad, gate_matrix, NT) + mm(up_pre_grad, up_matrix, NT)).astype(BF16)
    home_rows = over_experts(input_rows)
    token_grad = mm(home_rows, place, TN).astype(BF16)
    parts = token_grad.reshape(dp_count, width // dp_count, tok_count)
    heads = lax.all_to_all(parts, "dp", split_axis=0, concat_axis=0, tiled=True)
    input_grad = heads.transpose(0, 2, 1).reshape(1, dp_count * tok_count, width // dp_count)
    return (moe_out[None], input_grad, gate_grad[None])


def solution(mesh):
    in_specs = (
        P("expert", "dp", None),
        P("expert", "dp", None),
        P("expert", "dp"),
        P("expert", "dp"),
        P("expert", "dp", None),
        P("expert", "dp", None),
        P("expert", "dp", None),
    )
    out_specs = (P("expert", "dp", None), P("expert", None, "dp"), P("expert", "dp"))
    return jax.shard_map(local, mesh=mesh, in_specs=in_specs, out_specs=out_specs, check_vma=False)
```

time: 417 us -> 362 us (0.87)
  blocking collectives: 91.3 us -> 0 us
  waiting for transfers between devices: 224 us -> 260 us
  other arithmetic: 23.7 us -> 1.85 us
  starting transfers between devices: 7.35 us -> 24.1 us
  matrix products: 38.7 us -> 53.6 us
  local copies, waits for them, and re-layouts: 17.1 us -> 7.67 us
    all_to_all x3 -> x0, blocking collectives: 91.3 us -> none  [the longest x1 32.7 us: local(): lax.all_to_all(send_tokens, 'expert', split_axis=0, concat_axis=0, tiled=...]
    all_to_all x2 -> x6, waiting for transfers between devices: 50.1 us -> 78.8 us  [the longest x5 60.3 us: over_experts(): lax.all_to_all(rows.reshape(expert_count, capacity, cols), 'expert', spli...]
    unnamed x3 -> x0, other arithmetic: 19.7 us -> none
    all_to_all x2 -> x6, starting transfers between devices: 7.24 us -> 23.9 us  [the longest x5 20.4 us: over_experts(): lax.all_to_all(rows.reshape(expert_count, capacity, cols), 'expert', spli...]
    dot_general x6 -> x13, matrix products: 38.7 us -> 53.6 us  [mm(): return lax.dot_general(a, b, dims, preferred_element_type=F32)]
    gather x4 -> x0, local copies, waits for them, and re-layouts: 8.47 us -> none  [the longest x1 3.12 us: local(): jnp.concatenate([scaled_grad, zero_row])[slot_owner]]
    all_gather x3 -> x4, waiting for transfers between devices: 172 us -> 179 us  [the longest x1 68.7 us: local(): gate_matrix = lax.all_gather(w_gate, 'dp', axis=1, tiled=True)[0]]
  transfers between devices with their start and end apart: 5 -> 10, of which waited for: 5 -> 9; matrix products, arithmetic and copies ran while one was open for 5% -> 13% of each run, Pallas kernels for 0% -> 0%
where the time goes in v1:
time: 362 us; the launch traced here: 361 us
  waiting for transfers between devices  260 us (72%)
  matrix products  53.6 us (15%)
  starting transfers between devices  24.1 us (7%)
  between operations  14 us (4%)
  local copies, waits for them, and re-layouts  7.67 us (2%)
    all_gather x1, waiting for transfers between devices, local(): gate_matrix = lax.all_gather(w_gate, 'dp', axis=1, tiled=True)[0]  68.7 us
    all_gather x1, waiting for transfers between devices, local(): up_matrix = lax.all_gather(w_up, 'dp', axis=1, tiled=True)[0]  66.9 us
    all_to_all x5, waiting for transfers between devices, over_experts(): lax.all_to_all(rows.reshape(expert_count, capacity, cols), 'expert', spli...  60.3 us
    dot_general x13, matrix products, mm(): return lax.dot_general(a, b, dims, preferred_element_type=F32)  53.6 us
    all_gather x2, waiting for transfers between devices, local(): lax.all_gather(w_down[:, :, s], 'dp', axis=1, tiled=True)[0]  43.2 us
    all_to_all x5, starting transfers between devices, over_experts(): lax.all_to_all(rows.reshape(expert_count, capacity, cols), 'expert', spli...  20.4 us
    all_to_all x1, waiting for transfers between devices, local(): heads = lax.all_to_all(parts, 'dp', split_axis=0, concat_axis=0, tiled=True)  18.6 us
  transfers between devices with their start and end apart: 10, of which 9 were waited for; matrix products, arithmetic and copies ran while one was open for 13% of the time, Pallas kernels for 0%

profile of v1, /device:TPU:0, one launch (start us, length us, event | category | flops | bytes accessed | tf_op | source)
XLA Modules:
  0.0 360.8 jit_solution(10377897107065206636)
XLA Ops:
  7.2 2.2 fusion.51
  11.7 2.3 convolution_convert_fusion
  14.0 5.2 %all-to-all-start.3 = ((bf16[4,80,3584]{2,1,0:T(8,128)(2,1)}), bf16[4,80,3584]{2,1,0:T(8,128)(2,1)S(1)}, u32[]{:S(2)}, u32[]{:S(2)}) async-start(bf16[4,80,3584]{2,1,0:T(8,128)(2,1)} %bitcast.17), calls=%async_computation.3 | async-start | bytes 4587520 | tf_op jit(solution)/shard_map/all_to_all | solution.py:42
  21.3 24.9 %all-to-all-done.3 = bf16[4,80,3584]{2,1,0:T(8,128)(2,1)S(1)} async-done(((bf16[4,80,3584]{2,1,0:T(8,128)(2,1)}), bf16[4,80,3584]{2,1,0:T(8,128)(2,1)S(1)}, u32[]{:S(2)}, u32[]{:S(2)}) %all-to-all-start.3) | async-done | bytes 2293792 | tf_op jit(solution)/shard_map/all_to_all | solution.py:42
  47.6 3.6 %all-to-all-start = ((bf16[4,80,3584]{2,1,0:T(8,128)(2,1)}), bf16[4,80,3584]{2,1,0:T(8,128)(2,1)S(1)}, u32[]{:S(2)}, u32[]{:S(2)}) async-start(bf16[4,80,3584]{2,1,0:T(8,128)(2,1)} %bitcast.5), calls=%async_computation | async-start | bytes 4587520 | tf_op jit(solution)/shard_map/all_to_all | solution.py:42
  51.3 4.3 %all-gather.11.cloned.1.call-done = bf16[1,1024,1792]{2,1,0:T(8,128)(2,1)} async-done(((bf16[1,128,1792]{2,1,0:T(8,128)(2,1)}), bf16[1,1024,1792]{2,1,0:T(8,128)(2,1)}) %all-gather.11.cloned.1.call-update) | async-done | bytes 3670032 | tf_op jit(solution)/shard_map/all_gather | solution.py:53
  55.6 4.8 %fusion.14 = f32[320,1024]{1,0:T(8,128)} fusion(bf16[1,1024,1792]{2,1,0:T(8,128)(2,1)} %all-gather.11.cloned.1.call-done, bf16[320,3584]{1,0:T(8,128)(2,1)} %bitcast.80), kind=kOutput, calls=%fused_computation.13 | convolution fusion | flops 1174405120 | bytes 6127616 | tf_op jit(solution)/shard_map/dot_general | solution.py:22
  60.4 38.9 %all-gather.9.cloned.1.call-done = bf16[1,1024,1792]{2,1,0:T(8,128)(2,1)} async-done(((bf16[1,128,1792]{2,1,0:T(8,128)(2,1)}), bf16[1,1024,1792]{2,1,0:T(8,128)(2,1)}) %all-gather.9.cloned.1.call-update) | async-done | bytes 3670032 | tf_op jit(solution)/shard_map/all_gather | solution.py:53
  99.3 5.2 %fusion.28 = f32[320,1024]{1,0:T(8,128)} fusion(f32[320,1024]{1,0:T(8,128)} %fusion.14, bf16[1,1024,1792]{2,1,0:T(8,128)(2,1)} %all-gather.9.cloned.1.call-done, bf16[320,3584]{1,0:T(8,128)(2,1)} %bitcast.81), kind=kOutput, calls=%fused_computation.24 | convolution fusion | flops 1174732800 | bytes 7438336 | tf_op jit(solution)/shard_map/dot_general | solution.py:22
  104.5 68.7 %all-gather.5.cloned.1.call-done = bf16[1,3584,1024]{2,1,0:T(8,128)(2,1)} async-done(((bf16[1,448,1024]{2,1,0:T(8,128)(2,1)}), bf16[1,3584,1024]{2,1,0:T(8,128)(2,1)}) %all-gather.5.cloned.1.call-update) | async-done | bytes 7340048 | tf_op jit(solution)/shard_map/all_gather | solution.py:48
  173.2 6.7 %fusion.6 = f32[320,1024]{1,0:T(8,128)} fusion(bf16[320,3584]{1,0:T(8,128)(2,1)S(1)} %bitcast.78, bf16[1,3584,1024]{2,1,0:T(8,128)(2,1)} %all-gather.5.cloned.1.call-done), kind=kOutput, calls=%fused_computation.6 | convolution fusion | flops 2348810240 | bytes 10944512 | tf_op jit(solution)/shard_map/dot_general | solution.py:22
  179.9 66.9 %all-gather.7.cloned.1.call-done = bf16[1,3584,1024]{2,1,0:T(8,128)(2,1)} async-done(((bf16[1,448,1024]{2,1,0:T(8,128)(2,1)}), bf16[1,3584,1024]{2,1,0:T(8,128)(2,1)}) %all-gather.7.cloned.1.call-update) | async-done | bytes 7340048 | tf_op jit(solution)/shard_map/all_gather | solution.py:49
  246.8 7.2 %multiply_convert_fusion.3 = (bf16[320,1024]{1,0:T(8,128)(2,1)S(1)}, f32[320,1024]{1,0:T(8,128)}) fusion(f32[320,1024]{1,0:T(8,128)} %fusion.6, bf16[320,3584]{1,0:T(8,128)(2,1)S(1)} %bitcast.79, bf16[1,3584,1024]{2,1,0:T(8,128)(2,1)} %all-gather.7.cloned.1.call-done), kind=kOutput, calls=%fused_computation.27 | convolution fusion | flops 2350776320 | bytes 12910592 | tf_op jit(solution)/shard_map/dot_general | solution.py:22
  254.1 2.5 fusion.22
  256.5 3.7 %all-to-all-start.1 = ((bf16[4,80,1792]{2,1,0:T(8,128)(2,1)}), bf16[4,80,1792]{2,1,0:T(8,128)(2,1)S(1)}, u32[]{:S(2)}, u32[]{:S(2)}) async-start(bf16[4,80,1792]{2,1,0:T(8,128)(2,1)} %bitcast.10), calls=%async_computation.1 | async-start | bytes 2293760 | tf_op jit(solution)/shard_map/all_to_all | solution.py:42
  260.3 6.6 %fusion = f32[320,3584]{1,0:T(8,128)S(1)} fusion(bf16[1,3584,1024]{2,1,0:T(8,128)(2,1)} %all-gather.7.cloned.1.call-done, f32[320,1024]{1,0:T(8,128)} %fusion.28, f32[320,1024]{1,0:T(8,128)} %fusion.6), kind=kOutput, calls=%fused_computation | convolution fusion | flops 2350776320 | bytes 14548992 | tf_op jit(solution)/shard_map/dot_general | solution.py:22
  266.9 7.4 %fusion.11 = bf16[320,3584]{1,0:T(8,128)(2,1)} fusion(f32[320,3584]{1,0:T(8,128)S(1)} %fusion, bf16[1,3584,1024]{2,1,0:T(8,128)(2,1)} %all-gather.5.cloned.1.call-done, f32[320,1024]{1,0:T(8,128)S(1)} %copy-done.11, f32[320,1024]{1,0:T(8,128)S(1)} %copy-done.10, f32[320,1024]{1,0:T(8,128)S(1)} %copy-done.12), kind=kOutput, calls=%fused_computation.9 | convolution fusion | flops 2354380800 | bytes 18153472 | tf_op jit(solution)/shard_map/dot_general | solution.py:22
  276.4 3.6 %all-to-all-start.4 = ((bf16[4,80,3584]{2,1,0:T(8,128)(2,1)}), bf16[4,80,3584]{2,1,0:T(8,128)(2,1)S(1)}, u32[]{:S(2)}, u32[]{:S(2)}) async-start(bf16[4,80,3584]{2,1,0:T(8,128)(2,1)} %bitcast.82), calls=%async_computation.4 | async-start | bytes 4587520 | tf_op jit(solution)/shard_map/all_to_all | solution.py:42
  280.0 4.6 %fusion.25 = bf16[320,1792]{1,0:T(8,128)(2,1)} fusion(bf16[320,1024]{1,0:T(8,128)(2,1)} %copy-done.9, bf16[1,1024,1792]{2,1,0:T(8,128)(2,1)} %all-gather.11.cloned.1.call-done), kind=kOutput, calls=%fused_computation.22 | convolution fusion | flops 1174978560 | bytes 5472256 | tf_op jit(solution)/shard_map/dot_general | solution.py:22
  284.6 22.0 %all-to-all-done.4 = bf16[4,80,3584]{2,1,0:T(8,128)(2,1)S(1)} async-done(((bf16[4,80,3584]{2,1,0:T(8,128)(2,1)}), bf16[4,80,3584]{2,1,0:T(8,128)(2,1)S(1)}, u32[]{:S(2)}, u32[]{:S(2)}) %all-to-all-start.4) | async-done | bytes 2293792 | tf_op jit(solution)/shard_map/all_to_all | solution.py:42
  306.6 4.3 %all-to-all-start.2 = ((bf16[4,80,1792]{2,1,0:T(8,128)(2,1)}), bf16[4,80,1792]{2,1,0:T(8,128)(2,1)}, u32[]{:S(2)}, u32[]{:S(2)}) async-start(bf16[4,80,1792]{2,1,0:T(8,128)(2,1)} %bitcast.83), calls=%async_computation.2 | async-start | bytes 2293760 | tf_op jit(solution)/shard_map/all_to_all | solution.py:42
  312.8 12.3 %all-to-all-done.2 = bf16[4,80,1792]{2,1,0:T(8,128)(2,1)} async-done(((bf16[4,80,1792]{2,1,0:T(8,128)(2,1)}), bf16[4,80,1792]{2,1,0:T(8,128)(2,1)}, u32[]{:S(2)}, u32[]{:S(2)}) %all-to-all-start.2) | async-done | bytes 1146912 | tf_op jit(solution)/shard_map/all_to_all | solution.py:42
  325.1 3.6 all-to-all-start.5
  333.8 18.6 %all-to-all-done.5 = bf16[8,448,128]{2,1,0:T(8,128)(2,1)S(1)} async-done(((bf16[8,448,128]{2,1,0:T(8,128)(2,1)}), bf16[8,448,128]{2,1,0:T(8,128)(2,1)S(1)}, u32[]{:S(2)}, u32[]{:S(2)}) %all-to-all-start.5) | async-done | bytes 917536 | tf_op jit(solution)/shard_map/all_to_all | solution.py:83
  (47 shorter events, 16.8 us)
Async XLA Ops:
  7.2 12.0 %copy-start = (bf16[1,128,3584]{2,1,0:T(8,128)(2,1)S(1)}, bf16[1,128,3584]{2,1,0:T(8,128)(2,1)}, u32[]{:S(2)}) copy-start(bf16[1,128,3584]{2,1,0:T(8,128)(2,1)} %param.7) | copy-start | bytes 2752516
  7.2 48.4 %all-gather.11.cloned.1.call-start = ((), (), s32[]{:S(2)}) async-start(), calls=%async_computation.9 | async-start | bytes 4128768 | tf_op jit(solution)/shard_map/all_gather | solution.py:53
  9.4 2.1 copy-start.8
  9.4 2.3 copy-start.3
  9.4 2.3 copy-start.6
  9.5 89.8 %all-gather.9.cloned.1.call-start = ((), (), s32[]{:S(2)}) async-start(), calls=%async_computation.8 | async-start | bytes 4128768 | tf_op jit(solution)/shard_map/all_gather | solution.py:53
  10.2 163.0 %all-gather.5.cloned.1.call-start = ((), (), s32[]{:S(2)}) async-start(), calls=%async_computation.6 | async-start | bytes 8257536 | tf_op jit(solution)/shard_map/all_gather | solution.py:48
  10.9 235.9 %all-gather.7.cloned.1.call-start = ((), (), s32[]{:S(2)}) async-start(), calls=%async_computation.7 | async-start | bytes 8257536 | tf_op jit(solution)/shard_map/all_gather | solution.py:49
  14.0 32.1 %all-to-all-start.3 = ((bf16[4,80,3584]{2,1,0:T(8,128)(2,1)}), bf16[4,80,3584]{2,1,0:T(8,128)(2,1)S(1)}, u32[]{:S(2)}, u32[]{:S(2)}) async-start(bf16[4,80,3584]{2,1,0:T(8,128)(2,1)} %bitcast.17), calls=%async_computation.3 | async-start | bytes 4587520 | tf_op jit(solution)/shard_map/all_to_all | solution.py:42
  46.2 1.5 copy-start.5
  47.6 56.9 %all-to-all-start = ((bf16[4,80,3584]{2,1,0:T(8,128)(2,1)}), bf16[4,80,3584]{2,1,0:T(8,128)(2,1)S(1)}, u32[]{:S(2)}, u32[]{:S(2)}) async-start(bf16[4,80,3584]{2,1,0:T(8,128)(2,1)} %bitcast.5), calls=%async_computation | async-start | bytes 4587520 | tf_op jit(solution)/shard_map/all_to_all | solution.py:42
  246.8 7.2 %copy-start.7 = (bf16[1,1024,1792]{2,1,0:T(8,128)(2,1)S(1)}, bf16[1,1024,1792]{2,1,0:T(8,128)(2,1)}, u32[]{:S(2)}) copy-start(bf16[1,1024,1792]{2,1,0:T(8,128)(2,1)} %all-gather.9.cloned.1.call-done) | copy-start | bytes 11010052
  254.1 2.5 copy-start.9
  256.5 18.9 %all-to-all-start.1 = ((bf16[4,80,1792]{2,1,0:T(8,128)(2,1)}), bf16[4,80,1792]{2,1,0:T(8,128)(2,1)S(1)}, u32[]{:S(2)}, u32[]{:S(2)}) async-start(bf16[4,80,1792]{2,1,0:T(8,128)(2,1)} %bitcast.10), calls=%async_computation.1 | async-start | bytes 2293760 | tf_op jit(solution)/shard_map/all_to_all | solution.py:42
  260.2 6.6 %copy-start.10 = (f32[320,1024]{1,0:T(8,128)S(1)}, f32[320,1024]{1,0:T(8,128)}, u32[]{:S(2)}) copy-start(f32[320,1024]{1,0:T(8,128)} %fusion.28) | copy-start | bytes 3932164
  260.2 6.6 %copy-start.11 = (f32[320,1024]{1,0:T(8,128)S(1)}, f32[320,1024]{1,0:T(8,128)}, u32[]{:S(2)}) copy-start(f32[320,1024]{1,0:T(8,128)} %fusion.6) | copy-start | bytes 3932164
  260.2 6.6 %copy-start.12 = (f32[320,1024]{1,0:T(8,128)S(1)}, f32[320,1024]{1,0:T(8,128)}, u32[]{:S(2)}) copy-start(f32[320,1024]{1,0:T(8,128)} %get-tuple-element.10) | copy-start | bytes 3932164
  275.4 1.0 copy-start.1
  276.4 30.2 %all-to-all-start.4 = ((bf16[4,80,3584]{2,1,0:T(8,128)(2,1)}), bf16[4,80,3584]{2,1,0:T(8,128)(2,1)S(1)}, u32[]{:S(2)}, u32[]{:S(2)}) async-start(bf16[4,80,3584]{2,1,0:T(8,128)(2,1)} %bitcast.82), calls=%async_computation.4 | async-start | bytes 4587520 | tf_op jit(solution)/shard_map/all_to_all | solution.py:42
  306.6 18.5 %all-to-all-start.2 = ((bf16[4,80,1792]{2,1,0:T(8,128)(2,1)}), bf16[4,80,1792]{2,1,0:T(8,128)(2,1)}, u32[]{:S(2)}, u32[]{:S(2)}) async-start(bf16[4,80,1792]{2,1,0:T(8,128)(2,1)} %bitcast.83), calls=%async_computation.2 | async-start | bytes 2293760 | tf_op jit(solution)/shard_map/all_to_all | solution.py:42
  312.8 15.9 %copy-start.4 = (bf16[1,128,3584]{2,1,0:T(8,128)(2,1)S(1)}, bf16[1,128,3584]{2,1,0:T(8,128)(2,1)}, u32[]{:S(2)}) copy-start(bf16[1,128,3584]{2,1,0:T(8,128)(2,1)} %param.8) | copy-start | bytes 2752516
  325.1 27.3 %all-to-all-start.5 = ((bf16[8,448,128]{2,1,0:T(8,128)(2,1)}), bf16[8,448,128]{2,1,0:T(8,128)(2,1)S(1)}, u32[]{:S(2)}, u32[]{:S(2)}) async-start(bf16[8,448,128]{2,1,0:T(8,128)(2,1)} %bitcast.75), calls=%async_computation.5 | async-start | bytes 1835008 | tf_op jit(solution)/shard_map/all_to_all | solution.py:83
  328.6 1.3 copy-start.2
Sparse Core Ops, SparseCore 0:
  10.2 45.2 all-gather.10
  57.8 41.4 all-gather.8
  100.9 72.2 all-gather.4
  174.7 72.0 all-gather.6

commit v2 on v1

--- a/solution.py
+++ b/solution.py
@@ -1,11 +1,108 @@
+import functools
+
 import jax
 import jax.numpy as jnp
 from jax import lax
+from jax.experimental import pallas as pl
+from jax.experimental.pallas import tpu as pltpu
 from jax.sharding import PartitionSpec as P
 
 F32 = jnp.float32
 BF16 = jnp.bfloat16
-DOWN_PARTS = 2
+
+
+def gather_kernel(dp_count, *refs):
+    count = (len(refs) - 5) // 2
+    shards, wholes = refs[:count], refs[count : 2 * count]
+    right_sem, left_sem, pair_sem, recv_sem, own_sem = refs[2 * count :]
+    line = dp_count // 2
+    me = lax.axis_index("dp")
+    z, core = me // 2, me % 2
+    pair = z * 2 + (1 - core)
+    has_left, has_right = z > 0, z < line - 1
+
+    def greet(target):
+        pl.semaphore_signal(
+            barrier, inc=1, device_id={"dp": target}, device_id_type=pl.DeviceIdType.MESH
+        )
+
+    barrier = pltpu.get_barrier_semaphore()
+    greet(pair)
+    pl.when(has_left)(lambda: greet(me - 2))
+    pl.when(has_right)(lambda: greet(me + 2))
+    pl.semaphore_wait(barrier, 1 + has_left.astype(jnp.int32) + has_right.astype(jnp.int32))
+
+    def block(w, slot):
+        rows = shards[w].shape[0]
+        return wholes[w].at[pl.ds(pl.multiple_of(slot * rows, rows), rows)]
+
+    def copy(w, slot, sems, step, target, own=False):
+        return pltpu.make_async_remote_copy(
+            src_ref=shards[w] if own else block(w, slot),
+            dst_ref=block(w, slot),
+            send_sem=sems.at[w, step],
+            recv_sem=recv_sem.at[w, slot],
+            device_id={"dp": target},
+            device_id_type=pl.DeviceIdType.MESH,
+        )
+
+    for w in range(count):
+        pl.when(has_right)(lambda: copy(w, me, right_sem, 0, me + 2, True).start())
+        pl.when(has_left)(lambda: copy(w, me, left_sem, 0, me - 2, True).start())
+        copy(w, me, pair_sem, z, pair, True).start()
+        pltpu.make_async_copy(shards[w], block(w, me), own_sem.at[w]).start()
+
+    for step in range(1, line):
+        for w in range(count):
+            @pl.when(z >= step)
+            def _():
+                slot = me - 2 * step
+                copy(w, slot, pair_sem, z - step, pair).wait_recv()
+                pl.when(has_right)(lambda: copy(w, slot, right_sem, step, me + 2).start())
+                copy(w, slot, pair_sem, z - step, pair).start()
+
+            @pl.when(z + step < line)
+            def _():
+                slot = me + 2 * step
+                copy(w, slot, pair_sem, z + step, pair).wait_recv()
+                pl.when(has_left)(lambda: copy(w, slot, left_sem, step, me - 2).start())
+                copy(w, slot, pair_sem, z + step, pair).start()
+
+    for w in range(count):
+        pltpu.make_async_copy(shards[w], block(w, me), own_sem.at[w]).wait()
+        for other in range(line):
+            copy(w, other * 2 + 1 - core, pair_sem, other, pair).wait_recv()
+            copy(w, other * 2 + core, pair_sem, other, pair).wait_send()
+        for step in range(line):
+            pl.when(has_right & (z >= step))(
+                lambda: copy(w, me - 2 * step, right_sem, step, me + 2).wait_send()
+            )
+            pl.when(has_left & (z + step < line))(
+                lambda: copy(w, me + 2 * step, left_sem, step, me - 2).wait_send()
+            )
+
+
+def gather_weights(dp_count, shards):
+    count, line = len(shards), dp_count // 2
+    hbm = pl.BlockSpec(memory_space=pl.ANY)
+    moved = sum(x.size for x in shards) * 2 * dp_count
+    return pl.pallas_call(
+        functools.partial(gather_kernel, dp_count),
+        out_shape=[
+            jax.ShapeDtypeStruct((dp_count * x.shape[0], x.shape[1]), x.dtype) for x in shards
+        ],
+        in_specs=[hbm] * count,
+        out_specs=[hbm] * count,
+        scratch_shapes=[
+            pltpu.SemaphoreType.DMA((count, line)),
+            pltpu.SemaphoreType.DMA((count, line)),
+            pltpu.SemaphoreType.DMA((count, line)),
+            pltpu.SemaphoreType.DMA((count, dp_count)),
+            pltpu.SemaphoreType.DMA((count,)),
+        ],
+        cost_estimate=pl.CostEstimate(flops=0, bytes_accessed=moved * 25, transcendentals=0),
+        compiler_params=pltpu.CompilerParams(collective_id=3, has_side_effects=True),
+    )(*shards)
 
 
 def placement(route_line, expert_count, capacity):
@@ -45,39 +142,41 @@
         )
         return got.reshape(expert_count * capacity, cols)
 
-    gate_matrix = lax.all_gather(w_gate, "dp", axis=1, tiled=True)[0]
-    up_matrix = lax.all_gather(w_up, "dp", axis=1, tiled=True)[0]
-    w_down, _ = lax.optimization_barrier((w_down, gate_matrix[:16, :128]))
-    step = width // DOWN_PARTS
-    spans = [slice(i * step, (i + 1) * step) for i in range(DOWN_PARTS)]
-    downs = [lax.all_gather(w_down[:, :, s], "dp", axis=1, tiled=True)[0] for s in spans]
+    send = jnp.concatenate(
+        [
+            mm(place, rows).astype(BF16).reshape(expert_count, capacity, width)
+            for rows in (tokens[0], scaled_grad)
+        ],
+        axis=1,
+    )
+    arrived = lax.all_to_all(send, "expert", split_axis=0, concat_axis=0, tiled=True)
+    routed = arrived[:, :capacity].reshape(expert_count * capacity, width)
+    routed_grad = arrived[:, capacity:].reshape(expert_count * capacity, width)
 
-    routed = over_experts(mm(place, tokens[0]).astype(BF16))
-    routed_grad = over_experts(mm(place, scaled_grad).astype(BF16))
+    gate_matrix, up_matrix, down_matrix = gather_weights(
+        dp_count, (w_gate[0], w_up[0], w_down[0])
+    )
 
     gate_pre = mm(routed, gate_matrix)
     up_pre = mm(routed, up_matrix)
     sigmoid_gate = jax.nn.sigmoid(gate_pre)
     silu_gate = gate_pre * sigmoid_gate
     hidden = (silu_gate * up_pre).astype(BF16)
-
-    moe_parts = []
-    gate_grad = jnp.zeros((tok_count,), F32)
-    hidden_grad = jnp.zeros_like(gate_pre)
-    for s, down in zip(spans, downs):
-        expert_out = mm(hidden, down).astype(BF16)
-        hidden_grad = hidden_grad + mm(routed_grad[:, s], down, NT)
-        token_out = mm(place, over_experts(expert_out), TN)
-        moe_parts.append((gate_column * token_out).astype(BF16))
-        gate_grad = gate_grad + jnp.sum(own_grad[:, s] * token_out, axis=1)
-    moe_out = jnp.concatenate(moe_parts, axis=1)
+    expert_out = mm(hidden, down_matrix).astype(BF16)
+    hidden_grad = mm(routed_grad, down_matrix, NT)
+    expert_out, hidden_grad = lax.optimization_barrier((expert_out, hidden_grad))
+    returned = over_experts(expert_out)
 
     gate_pre_grad = (
         hidden_grad * up_pre * sigmoid_gate * (1.0 + gate_pre * (1.0 - sigmoid_gate))
     ).astype(BF16)
     up_pre_grad = (hidden_grad * silu_gate).astype(BF16)
     input_rows = (mm(gate_pre_grad, gate_matrix, NT) + mm(up_pre_grad, up_matrix, NT)).astype(BF16)
+    input_rows, returned = lax.optimization_barrier((input_rows, returned))
     home_rows = over_experts(input_rows)
+    token_out = mm(place, returned, TN)
+    moe_out = (gate_column * token_out).astype(BF16)
+    gate_grad = jnp.sum(own_grad * token_out, axis=1)
     token_grad = mm(home_rows, place, TN).astype(BF16)
     parts = token_grad.reshape(dp_count, width // dp_count, tok_count)
     heads = lax.all_to_all(parts, "dp", split_axis=0, concat_axis=0, tiled=True)

time: 362 us -> 312 us (0.86)
  waiting for transfers between devices: 260 us -> 33.5 us
  Pallas kernels: 0 us -> 185 us
  blocking collectives: 0 us -> 31.1 us
  matrix products: 53.6 us -> 37.4 us
  between operations: 14 us -> 0.84 us
  starting transfers between devices: 24.1 us -> 13.2 us
    pallas_call x0 -> x1, Pallas kernels: none -> 185 us  [gather_weights(): pl.pallas_call(functools.partial(gather_kernel, dp_count), out_shape=[jax...]
    all_gather x4 -> x0, waiting for transfers between devices: 179 us -> none  [the longest x1 68.7 us: local(): gate_matrix = lax.all_gather(w_gate, 'dp', axis=1, tiled=True)[0]]
    all_to_all x5 -> x1, waiting for transfers between devices: 60.3 us -> 13.2 us  [over_experts(): lax.all_to_all(rows.reshape(expert_count, capacity, cols), 'expert', spli...]
    all_to_all x0 -> x1, blocking collectives: none -> 31.1 us  [over_experts(): lax.all_to_all(rows.reshape(expert_count, capacity, cols), 'expert', spli...]
    all_to_all x5 -> x1, starting transfers between devices: 20.4 us -> 3.83 us  [over_experts(): lax.all_to_all(rows.reshape(expert_count, capacity, cols), 'expert', spli...]
    dot_general x13 -> x10, matrix products: 53.6 us -> 37.4 us  [mm(): return lax.dot_general(a, b, dims, preferred_element_type=F32)]
    all_to_all x0 -> x1, starting transfers between devices: none -> 5.16 us  [local(): lax.all_to_all(send, 'expert', split_axis=0, concat_axis=0, tiled=True)]
  transfers between devices with their start and end apart: 10 -> 3, of which waited for: 9 -> 2; matrix products, arithmetic and copies ran while one was open for 13% -> 6% of each run, Pallas kernels for 0% -> 59%
where the time goes in v2:
time: 312 us
  Pallas kernels  185 us (59%)
  matrix products  37.4 us (12%)
  waiting for transfers between devices  33.5 us (11%)
  blocking collectives  31.1 us (10%)
  starting transfers between devices  13.2 us (4%)
  local copies, waits for them, and re-layouts  6.36 us (2%)
  other arithmetic  4.06 us (1%)
    pallas_call x1, Pallas kernels, gather_weights(): pl.pallas_call(functools.partial(gather_kernel, dp_count), out_shape=[jax...  185 us
    dot_general x10, matrix products, mm(): return lax.dot_general(a, b, dims, preferred_element_type=F32)  37.4 us
    all_to_all x1, blocking collectives, over_experts(): lax.all_to_all(rows.reshape(expert_count, capacity, cols), 'expert', spli...  31.1 us
    all_to_all x1, waiting for transfers between devices, local(): heads = lax.all_to_all(parts, 'dp', split_axis=0, concat_axis=0, tiled=True)  20.3 us
    all_to_all x1, waiting for transfers between devices, over_experts(): lax.all_to_all(rows.reshape(expert_count, capacity, cols), 'expert', spli...  13.2 us
  transfers between devices with their start and end apart: 3, of which 2 were waited for; matrix products, arithmetic and copies ran while one was open for 6% of the time, Pallas kernels for 59%

profile of v2, /device:TPU:0, one launch (start us, length us, event | category | flops | bytes accessed | tf_op | source)
XLA Modules:
  0.0 311.7 jit_solution(15448269262193552284)
XLA Ops:
  0.6 0.9 convert_reduce_fusion
  1.6 0.7 fusion.19
  2.2 0.7 convolution_convert_fusion.2
  3.0 0.4 copy-done.2
  3.4 0.8 convolution_convert_fusion.1
  4.3 2.5 pad_maximum_fusion
  6.7 5.2 %all-to-all-start = ((bf16[4,160,3584]{2,1,0:T(8,128)(2,1)}), bf16[4,160,3584]{2,1,0:T(8,128)(2,1)}, u32[]{:S(2)}, u32[]{:S(2)}) async-start(bf16[4,160,3584]{2,1,0:T(8,128)(2,1)} %pad_maximum_fusion), calls=%async_computation | async-start | bytes 9175040 | tf_op jit(solution)/shard_map/all_to_all | solution.py:152
  11.9 185.2 %shard_map.94 = (bf16[3584,1024]{1,0:T(8,128)(2,1)}, bf16[3584,1024]{1,0:T(8,128)(2,1)}, bf16[1024,3584]{1,0:T(8,128)(2,1)}) custom-call(bf16[448,1024]{1,0:T(8,128)(2,1)} %bitcast.56, bf16[448,1024]{1,0:T(8,128)(2,1)} %bitcast.57, bf16[128,3584]{1,0:T(8,128)(2,1)} %bitcast.58), custom_call_target="tpu_custom_call" | custom-call | bytes 550502400 | tf_op jit(solution)/shard_map/pallas_call | solution.py:89
  197.1 2.8 fusion.23
  199.9 5.8 %fusion.24 = f32[320,1024]{1,0:T(8,128)S(1)} fusion(bf16[320,3584]{1,0:T(8,128)(2,1)S(1)} %bitcast.52, bf16[3584,1024]{1,0:T(8,128)(2,1)} %get-tuple-element.10), kind=kOutput, calls=%fused_computation.38 | convolution fusion | flops 2348810240 | bytes 10944512 | tf_op jit(solution)/shard_map/dot_general | solution.py:119
  205.7 2.7 fusion.25
  208.4 3.6 %fusion.26 = f32[320,1024]{1,0:T(8,128)} fusion(bf16[320,3584]{1,0:T(8,128)(2,1)S(1)} %bitcast.51, bf16[1024,3584]{1,0:T(8,128)(2,1)S(1)} %bitcast.65), kind=kOutput, calls=%fused_computation.40 | convolution fusion | flops 2348810240 | bytes 10944512 | tf_op jit(solution)/shard_map/dot_general | solution.py:119
  212.1 4.0 %convolution_convert_fusion = bf16[320,3584]{1,0:T(8,128)(2,1)} fusion(bf16[1024,3584]{1,0:T(8,128)(2,1)S(1)} %bitcast.65, f32[320,1024]{1,0:T(8,128)S(1)} %fusion.25, f32[320,1024]{1,0:T(8,128)S(1)} %fusion.24), kind=kOutput, calls=%fused_computation.2 | convolution fusion | flops 2351923200 | bytes 12255232 | tf_op jit(solution)/shard_map/dot_general | solution.py:119
  216.1 3.8 %all-to-all-start.1 = ((bf16[4,80,3584]{2,1,0:T(8,128)(2,1)}), bf16[4,80,3584]{2,1,0:T(8,128)(2,1)S(1)}, u32[]{:S(2)}, u32[]{:S(2)}) async-start(bf16[4,80,3584]{2,1,0:T(8,128)(2,1)} %bitcast.54), calls=%async_computation.1 | async-start | bytes 4587520 | tf_op jit(solution)/shard_map/all_to_all | solution.py:139
  219.9 7.2 %fusion.9 = f32[320,3584]{1,0:T(8,128)S(1)} fusion(bf16[3584,1024]{1,0:T(8,128)(2,1)} %get-tuple-element.10, f32[320,1024]{1,0:T(8,128)} %copy-done.4, f32[320,1024]{1,0:T(8,128)} %fusion.26, f32[320,1024]{1,0:T(8,128)} %copy-done.6), kind=kOutput, calls=%fused_computation.21 | convolution fusion | flops 2352087040 | bytes 15859712 | tf_op jit(solution)/shard_map/dot_general | solution.py:119
  227.1 7.2 %fusion = bf16[320,3584]{1,0:T(8,128)(2,1)} fusion(f32[320,3584]{1,0:T(8,128)S(1)} %fusion.9, bf16[3584,1024]{1,0:T(8,128)(2,1)} %get-tuple-element.11, f32[320,1024]{1,0:T(8,128)S(1)} %copy-done.7, f32[320,1024]{1,0:T(8,128)S(1)} %copy-done.5), kind=kOutput, calls=%fused_computation.1 | convolution fusion | flops 2353070080 | bytes 16842752 | tf_op jit(solution)/shard_map/dot_general | solution.py:119
  234.4 13.2 %all-to-all-done.1 = bf16[4,80,3584]{2,1,0:T(8,128)(2,1)S(1)} async-done(((bf16[4,80,3584]{2,1,0:T(8,128)(2,1)}), bf16[4,80,3584]{2,1,0:T(8,128)(2,1)S(1)}, u32[]{:S(2)}, u32[]{:S(2)}) %all-to-all-start.1) | async-done | bytes 2293792 | tf_op jit(solution)/shard_map/all_to_all | solution.py:139
  247.6 31.1 %all_to_all.20 = bf16[4,80,3584]{2,1,0:T(8,128)(2,1)S(1)} all-to-all(bf16[4,80,3584]{2,1,0:T(8,128)(2,1)} %bitcast.55), channel_id=1, replica_groups=mesh['dp'=8,'expert'=4] {'expert'}, dimensions={0} | all-to-all | bytes 4587520 | tf_op jit(solution)/shard_map/all_to_all | solution.py:139
  278.7 1.9 convolution_convert_fusion.3
  280.5 4.2 %all-to-all-start.3 = ((bf16[8,448,128]{2,1,0:T(8,128)(2,1)}), bf16[8,448,128]{2,1,0:T(8,128)(2,1)}, u32[]{:S(2)}, u32[]{:S(2)}) async-start(bf16[8,448,128]{2,1,0:T(8,128)(2,1)} %bitcast.18), calls=%async_computation.3 | async-start | bytes 1835008 | tf_op jit(solution)/shard_map/all_to_all | solution.py:182
  284.8 3.5 %fusion.2 = (f32[128]{0:T(128)}, bf16[1,128,3584]{2,1,0:T(8,128)(2,1)}) fusion(bf16[1,128,3584]{2,1,0:T(8,128)(2,1)} %param.8, f32[128]{0:T(128)S(1)} %bitcast.60, bf16[320,3584]{1,0:T(8,128)(2,1)S(1)} %bitcast.50, s32[128]{0:T(128)S(1)} %fusion.19), kind=kOutput, calls=%fused_computation.10 | convolution fusion | flops 295935872 | bytes 4130304 | tf_op jit(solution)/shard_map/dot_general | solution.py:119
  288.3 20.3 %all-to-all-done.3 = bf16[8,448,128]{2,1,0:T(8,128)(2,1)} async-done(((bf16[8,448,128]{2,1,0:T(8,128)(2,1)}), bf16[8,448,128]{2,1,0:T(8,128)(2,1)}, u32[]{:S(2)}, u32[]{:S(2)}) %all-to-all-start.3) | async-done | bytes 917536 | tf_op jit(solution)/shard_map/all_to_all | solution.py:182
  308.6 1.8 copy.11
  310.3 1.3 reshape.50
  (26 shorter events, 0.1 us)
Async XLA Ops:
  0.6 1.6 copy-start
  2.2 1.2 copy-start.2
  2.2 1.2 copy-start.3
  6.7 190.3 %all-to-all-start = ((bf16[4,160,3584]{2,1,0:T(8,128)(2,1)}), bf16[4,160,3584]{2,1,0:T(8,128)(2,1)}, u32[]{:S(2)}, u32[]{:S(2)}) async-start(bf16[4,160,3584]{2,1,0:T(8,128)(2,1)} %pad_maximum_fusion), calls=%async_computation | async-start | bytes 9175040 | tf_op jit(solution)/shard_map/all_to_all | solution.py:152
  197.1 8.6 %slice-start = ((s8[7340032]{0:T(1024)(128)(4,1)}), s8[4194304]{0:T(1024)(128)(4,1)S(1)}, s32[]{:S(2)}) async-start(s8[7340032]{0:T(1024)(128)(4,1)} %bitcast.62), calls=%async_computation.4 | async-start | bytes 8388608
  199.9 5.8 %slice-start.1 = ((s8[7340032]{0:T(1024)(128)(4,1)}), s8[3145728]{0:T(1024)(128)(4,1)S(1)}, s32[]{:S(2)}) async-start(s8[7340032]{0:T(1024)(128)(4,1)} %bitcast.62), calls=%async_computation.5 | async-start | bytes 6291456
  199.9 8.5 %slice-start.2 = ((s8[7340032]{0:T(1024)(128)(4,1)}), s8[4194304]{0:T(1024)(128)(4,1)S(1)}, s32[]{:S(2)}) async-start(s8[7340032]{0:T(1024)(128)(4,1)} %bitcast.64), calls=%async_computation.6 | async-start | bytes 8388608
  205.7 6.4 %copy-start.4 = (f32[320,1024]{1,0:T(8,128)}, f32[320,1024]{1,0:T(8,128)S(1)}, u32[]{:S(2)}) copy-start(f32[320,1024]{1,0:T(8,128)S(1)} %fusion.24) | copy-start | bytes 3932164
  205.7 2.7 slice-start.3
  208.4 3.7 %copy-start.6 = (f32[320,1024]{1,0:T(8,128)}, f32[320,1024]{1,0:T(8,128)S(1)}, u32[]{:S(2)}) copy-start(f32[320,1024]{1,0:T(8,128)S(1)} %fusion.25) | copy-start | bytes 3932164
  216.1 31.5 %all-to-all-start.1 = ((bf16[4,80,3584]{2,1,0:T(8,128)(2,1)}), bf16[4,80,3584]{2,1,0:T(8,128)(2,1)S(1)}, u32[]{:S(2)}, u32[]{:S(2)}) async-start(bf16[4,80,3584]{2,1,0:T(8,128)(2,1)} %bitcast.54), calls=%async_computation.1 | async-start | bytes 4587520 | tf_op jit(solution)/shard_map/all_to_all | solution.py:139
  219.9 7.2 %copy-start.5 = (f32[320,1024]{1,0:T(8,128)S(1)}, f32[320,1024]{1,0:T(8,128)}, u32[]{:S(2)}) copy-start(f32[320,1024]{1,0:T(8,128)} %copy-done.4) | copy-start | bytes 3932164
  219.9 7.2 %copy-start.7 = (f32[320,1024]{1,0:T(8,128)S(1)}, f32[320,1024]{1,0:T(8,128)}, u32[]{:S(2)}) copy-start(f32[320,1024]{1,0:T(8,128)} %fusion.26) | copy-start | bytes 3932164
  280.5 28.0 %all-to-all-start.3 = ((bf16[8,448,128]{2,1,0:T(8,128)(2,1)}), bf16[8,448,128]{2,1,0:T(8,128)(2,1)}, u32[]{:S(2)}, u32[]{:S(2)}) async-start(bf16[8,448,128]{2,1,0:T(8,128)(2,1)} %bitcast.18), calls=%async_computation.3 | async-start | bytes 1835008 | tf_op jit(solution)/shard_map/all_to_all | solution.py:182
  284.8 26.9 %copy-start.1 = (bf16[1,128,3584]{2,1,0:T(8,128)(2,1)S(1)}, bf16[1,128,3584]{2,1,0:T(8,128)(2,1)}, u32[]{:S(2)}) copy-start(bf16[1,128,3584]{2,1,0:T(8,128)(2,1)} %param.7) | copy-start | bytes 2752516

commit v3 on v2

--- a/solution.py
+++ b/solution.py
@@ -123,6 +123,132 @@
 TN = (((0,), (0,)), ((), ()))
 
 
+def heads_kernel(expert_count, dp_count, rows, place, out, got, turned, *sems):
+    row_sem, got_sem, own_sem, turn_sem, head_sem, keep_sem = sems
+    expert, me = lax.axis_index("expert"), lax.axis_index("dp")
+    chunks, cols = got.shape[0], got.shape[3]
+    depth, tok_count = out.shape[0], place.shape[2]
+    per = cols // depth
+    mesh_type = pl.DeviceIdType.MESH
+
+    barrier = pltpu.get_barrier_semaphore()
+    for o in range(1, expert_count):
+        pl.semaphore_signal(
+            barrier, inc=1, device_id={"expert": (expert + o) % expert_count},
+            device_id_type=mesh_type,
+        )
+    for o in range(1, dp_count):
+        pl.semaphore_signal(
+            barrier, inc=1, device_id={"dp": (me + o) % dp_count}, device_id_type=mesh_type
+        )
+    pl.semaphore_wait(barrier, expert_count + dp_count - 2)
+
+    def chunk_of(i):
+        return (me // per + 1 + i) % chunks
+
+    def source(k, e):
+        return rows.at[e, :, pl.ds(pl.multiple_of(k * cols, 128), cols)]
+
+    def give(i, target, slot):
+        k = chunk_of(i)
+        return pltpu.make_async_remote_copy(
+            src_ref=source(k, target), dst_ref=got.at[k, slot],
+            send_sem=row_sem.at[i, target], recv_sem=got_sem.at[i, slot],
+            device_id={"expert": target}, device_id_type=mesh_type,
+        )
+
+    def keep(i):
+        k = chunk_of(i)
+        return pltpu.make_async_copy(source(k, expert), got.at[k, expert], own_sem.at[i])
+
+    def column(slot):
+        return out.at[:, pl.ds(pl.multiple_of(slot * tok_count, 128), tok_count)]
+
+    def hand(i, p, target, slot):
+        return pltpu.make_async_remote_copy(
+            src_ref=turned.at[i, pl.ds(p * depth, depth)], dst_ref=column(slot),
+            send_sem=turn_sem.at[i, p], recv_sem=head_sem.at[slot],
+            device_id={"dp": target}, device_id_type=mesh_type,
+        )
+
+    def stay(p):
+        return pltpu.make_async_copy(
+            turned.at[chunks - 1, pl.ds(p * depth, depth)], column(me), keep_sem
+        )
+
+    for i in range(chunks):
+        keep(i).start()
+        for o in range(1, expert_count):
+            give(i, (expert + o) % expert_count, expert).start()
+
+    for i in range(chunks):
+        k = chunk_of(i)
+        keep(i).wait()
+        for o in range(1, expert_count):
+            peer = (expert + o) % expert_count
+            give(i, peer, peer).wait_recv()
+        total = jnp.zeros((cols, tok_count), F32)
+        for e in range(expert_count):
+            total = total + mm(got[k, e], place[e], TN)
+        turned[i] = total.astype(BF16)
+        for p in range(per):
+            target = k * per + p
+            if i < chunks - 1:
+                hand(i, p, target, me).start()
+            else:
+                pl.when(me % per != p)(lambda: hand(i, p, target, me).start())
+                pl.when(me % per == p)(lambda: stay(p).start())
+
+    for i in range(chunks):
+        k = chunk_of(i)
+        for o in range(1, expert_count):
+            give(i, (expert + o) % expert_count, expert).wait_send()
+        for p in range(per):
+            target = k * per + p
+            if i < chunks - 1:
+                hand(i, p, target, me).wait_send()
+            else:
+                pl.when(me % per != p)(lambda: hand(i, p, target, me).wait_send())
+                pl.when(me % per == p)(lambda: stay(p).wait())
+    for o in range(1, dp_count):
+        peer = (me + o) % dp_count
+        hand(0, 0, peer, peer).wait_recv()
+
+
+def to_heads(expert_count, dp_count, rows, place):
+    _, capacity, width = rows.shape
+    tok_count = place.shape[2]
+    chunks = 4
+    cols, depth = width // chunks, width // dp_count
+    per = cols // depth
+    dma = pltpu.SemaphoreType.DMA
+    return pl.pallas_call(
+        functools.partial(heads_kernel, expert_count, dp_count),
+        out_shape=jax.ShapeDtypeStruct((depth, dp_count * tok_count), BF16),
+        in_specs=[
+            pl.BlockSpec(memory_space=pl.ANY),
+            pl.BlockSpec(memory_space=pltpu.VMEM),
+        ],
+        out_specs=pl.BlockSpec(memory_space=pl.ANY),
+        scratch_shapes=[
+            pltpu.VMEM((chunks, expert_count, capacity, cols), BF16),
+            pltpu.VMEM((chunks, cols, tok_count), BF16),
+            dma((chunks, expert_count)),
+            dma((chunks, expert_count)),
+            dma((chunks,)),
+            dma((chunks, per)),
+            dma((dp_count,)),
+            dma,
+        ],
+        cost_estimate=pl.CostEstimate(
+            flops=2 * rows.size * tok_count, bytes_accessed=60 * rows.size, transcendentals=0
+        ),
+        compiler_params=pltpu.CompilerParams(
+            collective_id=5, has_side_effects=True, vmem_limit_bytes=32 * 1024 * 1024
+        ),
+    )(rows, place)
+
+
 def local(tokens, grad_out, route_ids, route_gates, w_gate, w_up, w_down):
     expert_count = lax.axis_size("expert")
     dp_count = lax.axis_size("dp")
@@ -172,15 +298,16 @@
     ).astype(BF16)
     up_pre_grad = (hidden_grad * silu_gate).astype(BF16)
     input_rows = (mm(gate_pre_grad, gate_matrix, NT) + mm(up_pre_grad, up_matrix, NT)).astype(BF16)
-    input_rows, returned = lax.optimization_barrier((input_rows, returned))
-    home_rows = over_experts(input_rows)
+    heads = to_heads(
+        expert_count,
+        dp_count,
+        input_rows.reshape(expert_count, capacity, width),
+        place.reshape(expert_count, capacity, tok_count),
+    )
+    input_grad = heads.T[None]
     token_out = mm(place, returned, TN)
     moe_out = (gate_column * token_out).astype(BF16)
     gate_grad = jnp.sum(own_grad * token_out, axis=1)
-    token_grad = mm(home_rows, place, TN).astype(BF16)
-    parts = token_grad.reshape(dp_count, width // dp_count, tok_count)
-    heads = lax.all_to_all(parts, "dp", split_axis=0, concat_axis=0, tiled=True)
-    input_grad = heads.transpose(0, 2, 1).reshape(1, dp_count * tok_count, width // dp_count)
     return (moe_out[None], input_grad, gate_grad[None])
 
 

time: 312 us -> 281 us (0.901)
  Pallas kernels: 185 us -> 227 us
  waiting for transfers between devices: 33.5 us -> 0.01 us
  blocking collectives: 31.1 us -> 0 us
  starting transfers between devices: 13.2 us -> 9.84 us
  matrix products: 37.4 us -> 34.1 us
    pallas_call x0 -> x1, Pallas kernels: none -> 42.1 us  [to_heads(): pl.pallas_call(functools.partial(heads_kernel, expert_count, dp_count), o...]
    all_to_all x1 -> x0, blocking collectives: 31.1 us -> none  [over_experts(): lax.all_to_all(rows.reshape(expert_count, capacity, cols), 'expert', spli...]
    all_to_all x1 -> x0, waiting for transfers between devices: 20.3 us -> none  [local(): heads = lax.all_to_all(parts, 'dp', split_axis=0, concat_axis=0, tiled=True)]
    all_to_all x1, waiting for transfers between devices: 13.2 us -> 0.01 us  [over_experts(): lax.all_to_all(rows.reshape(expert_count, capacity, cols), 'expert', spli...]
    all_to_all x1 -> x0, starting transfers between devices: 4.24 us -> none  [local(): heads = lax.all_to_all(parts, 'dp', split_axis=0, concat_axis=0, tiled=True)]
    dot_general x10 -> x9, matrix products: 37.4 us -> 34.1 us  [mm(): return lax.dot_general(a, b, dims, preferred_element_type=F32)]
  transfers between devices with their start and end apart: 3 -> 2, of which waited for: 2 -> 0; matrix products, arithmetic and copies ran while one was open for 6% -> 4% of each run, Pallas kernels for 59% -> 81%
where the time goes in v3:
time: 281 us; the launch traced here: 280 us
  Pallas kernels  227 us (81%)
  matrix products  34.1 us (12%)
  starting transfers between devices  9.84 us (4%)
  other arithmetic  4.2 us (1%)
  local copies, waits for them, and re-layouts  4.18 us (1%)
    pallas_call x1, Pallas kernels, gather_weights(): pl.pallas_call(functools.partial(gather_kernel, dp_count), out_shape=[jax...  185 us
    pallas_call x1, Pallas kernels, to_heads(): pl.pallas_call(functools.partial(heads_kernel, expert_count, dp_count), o...  42.1 us
    dot_general x9, matrix products, mm(): return lax.dot_general(a, b, dims, preferred_element_type=F32)  34.1 us
  transfers between devices with their start and end apart: 2, of which 0 were waited for; matrix products, arithmetic and copies ran while one was open for 4% of the time, Pallas kernels for 81%

profile of v3, /device:TPU:0, one launch (start us, length us, event | category | flops | bytes accessed | tf_op | source)
XLA Modules:
  0.0 280.4 jit_solution(15019526024107682165)
XLA Ops:
  0.6 0.0 copy-start
  0.6 0.9 convert_reduce_fusion
  1.6 0.7 fusion.18
  2.2 0.7 convolution_convert_fusion.2
  3.0 0.4 copy-done.1
  3.4 0.8 convolution_convert_fusion.1
  4.3 2.5 pad_maximum_fusion
  6.8 5.2 %all-to-all-start = ((bf16[4,160,3584]{2,1,0:T(8,128)(2,1)}), bf16[4,160,3584]{2,1,0:T(8,128)(2,1)}, u32[]{:S(2)}, u32[]{:S(2)}) async-start(bf16[4,160,3584]{2,1,0:T(8,128)(2,1)} %pad_maximum_fusion), calls=%async_computation | async-start | bytes 9175040 | tf_op jit(solution)/shard_map/all_to_all | solution.py:278
  11.9 185.2 %shard_map.94 = (bf16[3584,1024]{1,0:T(8,128)(2,1)}, bf16[3584,1024]{1,0:T(8,128)(2,1)}, bf16[1024,3584]{1,0:T(8,128)(2,1)}) custom-call(bf16[448,1024]{1,0:T(8,128)(2,1)} %bitcast.52, bf16[448,1024]{1,0:T(8,128)(2,1)} %bitcast.53, bf16[128,3584]{1,0:T(8,128)(2,1)} %bitcast.54), custom_call_target="tpu_custom_call" | custom-call | bytes 550502400 | tf_op jit(solution)/shard_map/pallas_call | solution.py:89
  197.1 0.1 compare_convert_fusion.place
  197.2 0.0 slice-start
  197.3 2.8 fusion.22
  200.0 0.0 slice-start.1
  200.1 5.8 %fusion.23 = f32[320,1024]{1,0:T(8,128)S(1)} fusion(bf16[320,3584]{1,0:T(8,128)(2,1)S(1)} %bitcast.49, bf16[3584,1024]{1,0:T(8,128)(2,1)} %get-tuple-element.8), kind=kOutput, calls=%fused_computation.38 | convolution fusion | flops 2348810240 | bytes 10944512 | tf_op jit(solution)/shard_map/dot_general | solution.py:119
  205.9 2.7 fusion.24
  208.6 3.6 %fusion.25 = f32[320,1024]{1,0:T(8,128)} fusion(bf16[320,3584]{1,0:T(8,128)(2,1)S(1)} %bitcast.48, bf16[1024,3584]{1,0:T(8,128)(2,1)S(1)} %bitcast.61), kind=kOutput, calls=%fused_computation.40 | convolution fusion | flops 2348810240 | bytes 10944512 | tf_op jit(solution)/shard_map/dot_general | solution.py:119
  212.2 4.1 %convolution_convert_fusion = bf16[320,3584]{1,0:T(8,128)(2,1)} fusion(bf16[1024,3584]{1,0:T(8,128)(2,1)S(1)} %bitcast.61, f32[320,1024]{1,0:T(8,128)S(1)} %fusion.24, f32[320,1024]{1,0:T(8,128)S(1)} %fusion.23), kind=kOutput, calls=%fused_computation.2 | convolution fusion | flops 2351923200 | bytes 12255232 | tf_op jit(solution)/shard_map/dot_general | solution.py:119
  216.3 4.7 %all-to-all-start.1 = ((bf16[4,80,3584]{2,1,0:T(8,128)(2,1)}), bf16[4,80,3584]{2,1,0:T(8,128)(2,1)}, u32[]{:S(2)}, u32[]{:S(2)}) async-start(bf16[4,80,3584]{2,1,0:T(8,128)(2,1)} %bitcast.51), calls=%async_computation.1 | async-start | bytes 4587520 | tf_op jit(solution)/shard_map/all_to_all | solution.py:265
  221.0 6.8 %fusion.9 = f32[320,3584]{1,0:T(8,128)S(1)} fusion(bf16[3584,1024]{1,0:T(8,128)(2,1)} %get-tuple-element.8, f32[320,1024]{1,0:T(8,128)S(1)} %fusion.23, f32[320,1024]{1,0:T(8,128)} %fusion.25, f32[320,1024]{1,0:T(8,128)} %copy-done.3), kind=kOutput, calls=%fused_computation.20 | convolution fusion | flops 2352087040 | bytes 15859712 | tf_op jit(solution)/shard_map/dot_general | solution.py:119
  227.8 5.7 %fusion = bf16[320,3584]{1,0:T(8,128)(2,1)S(1)} fusion(f32[320,3584]{1,0:T(8,128)S(1)} %fusion.9, bf16[3584,1024]{1,0:T(8,128)(2,1)} %get-tuple-element.9, f32[320,1024]{1,0:T(8,128)S(1)} %copy-done.4, f32[320,1024]{1,0:T(8,128)S(1)} %fusion.23), kind=kOutput, calls=%fused_computation.1 | convolution fusion | flops 2353070080 | bytes 16842752 | tf_op jit(solution)/shard_map/dot_general | solution.py:119
  233.5 42.1 %shard_map.95 = bf16[448,1024]{1,0:T(8,128)(2,1)S(1)} custom-call(bf16[4,80,3584]{2,1,0:T(8,128)(2,1)S(1)} %bitcast.45, bf16[4,80,128]{2,1,0:T(8,128)(2,1)S(1)} %compare_convert_fusion.place), custom_call_target="tpu_custom_call" | custom-call | flops 293601280 | bytes 68812800 | tf_op jit(solution)/shard_map/pallas_call | solution.py:225
  275.6 0.0 all-to-all-done.1
  275.6 3.9 %fusion.2 = (f32[128]{0:T(128)}, bf16[1,128,3584]{2,1,0:T(8,128)(2,1)}) fusion(bf16[1,128,3584]{2,1,0:T(8,128)(2,1)S(1)} %copy-done.1, f32[128]{0:T(128)S(1)} %bitcast.56, bf16[320,3584]{1,0:T(8,128)(2,1)} %bitcast.14, s32[128]{0:T(128)S(1)} %fusion.18), kind=kOutput, calls=%fused_computation.9 | convolution fusion | flops 295935872 | bytes 4130304 | tf_op jit(solution)/shard_map/dot_general | solution.py:119
  279.5 0.9 copy.11
  (18 shorter events, 0.0 us)
Async XLA Ops:
  0.6 1.6 copy-start
  2.2 1.2 copy-start.1
  2.2 1.2 copy-start.2
  6.8 190.5 %all-to-all-start = ((bf16[4,160,3584]{2,1,0:T(8,128)(2,1)}), bf16[4,160,3584]{2,1,0:T(8,128)(2,1)}, u32[]{:S(2)}, u32[]{:S(2)}) async-start(bf16[4,160,3584]{2,1,0:T(8,128)(2,1)} %pad_maximum_fusion), calls=%async_computation | async-start | bytes 9175040 | tf_op jit(solution)/shard_map/all_to_all | solution.py:278
  197.2 8.6 %slice-start = ((s8[7340032]{0:T(1024)(128)(4,1)}), s8[4194304]{0:T(1024)(128)(4,1)S(1)}, s32[]{:S(2)}) async-start(s8[7340032]{0:T(1024)(128)(4,1)} %bitcast.58), calls=%async_computation.2 | async-start | bytes 8388608
  200.0 5.8 %slice-start.1 = ((s8[7340032]{0:T(1024)(128)(4,1)}), s8[3145728]{0:T(1024)(128)(4,1)S(1)}, s32[]{:S(2)}) async-start(s8[7340032]{0:T(1024)(128)(4,1)} %bitcast.58), calls=%async_computation.3 | async-start | bytes 6291456
  200.1 8.5 %slice-start.2 = ((s8[7340032]{0:T(1024)(128)(4,1)}), s8[4194304]{0:T(1024)(128)(4,1)S(1)}, s32[]{:S(2)}) async-start(s8[7340032]{0:T(1024)(128)(4,1)} %bitcast.60), calls=%async_computation.4 | async-start | bytes 8388608
  205.9 2.7 slice-start.3
  208.5 3.7 %copy-start.3 = (f32[320,1024]{1,0:T(8,128)}, f32[320,1024]{1,0:T(8,128)S(1)}, u32[]{:S(2)}) copy-start(f32[320,1024]{1,0:T(8,128)S(1)} %fusion.24) | copy-start | bytes 3932164
  216.3 59.3 %all-to-all-start.1 = ((bf16[4,80,3584]{2,1,0:T(8,128)(2,1)}), bf16[4,80,3584]{2,1,0:T(8,128)(2,1)}, u32[]{:S(2)}, u32[]{:S(2)}) async-start(bf16[4,80,3584]{2,1,0:T(8,128)(2,1)} %bitcast.51), calls=%async_computation.1 | async-start | bytes 4587520 | tf_op jit(solution)/shard_map/all_to_all | solution.py:265
  221.0 6.8 %copy-start.4 = (f32[320,1024]{1,0:T(8,128)S(1)}, f32[320,1024]{1,0:T(8,128)}, u32[]{:S(2)}) copy-start(f32[320,1024]{1,0:T(8,128)} %fusion.25) | copy-start | bytes 3932164

commit v4 on v3

--- a/solution.py
+++ b/solution.py
@@ -11,10 +11,14 @@
 BF16 = jnp.bfloat16
 
 
-def gather_kernel(dp_count, *refs):
-    count = (len(refs) - 5) // 2
-    shards, wholes = refs[:count], refs[count : 2 * count]
-    right_sem, left_sem, pair_sem, recv_sem, own_sem = refs[2 * count :]
+def gather_kernel(dp_count, expert_count, count, kinds, *refs):
+    shards, sent = refs[:count], refs[count : count + kinds]
+    refs = refs[count + kinds :]
+    wholes, got = refs[:count], refs[count : count + kinds]
+    right_sem, left_sem, pair_sem, recv_sem, own_sem, give_sem, got_sem, keep_sem = refs[
+        count + kinds :
+    ]
+    expert = lax.axis_index("expert")
     line = dp_count // 2
     me = lax.axis_index("dp")
     z, core = me // 2, me % 2
@@ -30,7 +34,12 @@
     greet(pair)
     pl.when(has_left)(lambda: greet(me - 2))
     pl.when(has_right)(lambda: greet(me + 2))
-    pl.semaphore_wait(barrier, 1 + has_left.astype(jnp.int32) + has_right.astype(jnp.int32))
+    for o in range(1, expert_count):
+        pl.semaphore_signal(
+            barrier, inc=1, device_id={"expert": (expert + o) % expert_count},
+            device_id_type=pl.DeviceIdType.MESH,
+        )
+    pl.semaphore_wait(barrier, expert_count + has_left.astype(jnp.int32) + has_right.astype(jnp.int32))
 
     def block(w, slot):
         rows = shards[w].shape[0]
@@ -51,6 +60,26 @@
         pl.when(has_left)(lambda: copy(w, me, left_sem, 0, me - 2, True).start())
         copy(w, me, pair_sem, z, pair, True).start()
         pltpu.make_async_copy(shards[w], block(w, me), own_sem.at[w]).start()
+
+    def give(kind, target, slot):
+        return pltpu.make_async_remote_copy(
+            src_ref=sent[kind].at[target],
+            dst_ref=got[kind].at[slot],
+            send_sem=give_sem.at[kind, target],
+            recv_sem=got_sem.at[kind, slot],
+            device_id={"expert": target},
+            device_id_type=pl.DeviceIdType.MESH,
+        )
+
+    def keep(kind):
+        return pltpu.make_async_copy(
+            sent[kind].at[expert], got[kind].at[expert], keep_sem.at[kind]
+        )
+
+    for kind in range(kinds):
+        keep(kind).start()
+        for o in range(1, expert_count):
+            give(kind, (expert + o) % expert_count, expert).start()
 
     for step in range(1, line):
         for w in range(count):
@@ -80,29 +109,39 @@
             pl.when(has_left & (z + step < line))(
                 lambda: copy(w, me + 2 * step, left_sem, step, me - 2).wait_send()
             )
-
-
-def gather_weights(dp_count, shards):
-    count, line = len(shards), dp_count // 2
+    for kind in range(kinds):
+        keep(kind).wait()
+        for o in range(1, expert_count):
+            peer = (expert + o) % expert_count
+            give(kind, peer, expert).wait_send()
+            give(kind, peer, peer).wait_recv()
+
+
+def gather_weights(dp_count, expert_count, shards, sent):
+    count, line, kinds = len(shards), dp_count // 2, len(sent)
     hbm = pl.BlockSpec(memory_space=pl.ANY)
     moved = sum(x.size for x in shards) * 2 * dp_count
     return pl.pallas_call(
-        functools.partial(gather_kernel, dp_count),
+        functools.partial(gather_kernel, dp_count, expert_count, count, kinds),
         out_shape=[
             jax.ShapeDtypeStruct((dp_count * x.shape[0], x.shape[1]), x.dtype) for x in shards
-        ],
-        in_specs=[hbm] * count,
-        out_specs=[hbm] * count,
+        ]
+        + [jax.ShapeDtypeStruct(x.shape, x.dtype) for x in sent],
+        in_specs=[hbm] * (count + kinds),
+        out_specs=[hbm] * (count + kinds),
         scratch_shapes=[
             pltpu.SemaphoreType.DMA((count, line)),
             pltpu.SemaphoreType.DMA((count, line)),
             pltpu.SemaphoreType.DMA((count, line)),
             pltpu.SemaphoreType.DMA((count, dp_count)),
             pltpu.SemaphoreType.DMA((count,)),
+            pltpu.SemaphoreType.DMA((kinds, expert_count)),
+            pltpu.SemaphoreType.DMA((kinds, expert_count)),
+            pltpu.SemaphoreType.DMA((kinds,)),
         ],
         cost_estimate=pl.CostEstimate(flops=0, bytes_accessed=moved * 25, transcendentals=0),
         compiler_params=pltpu.CompilerParams(collective_id=3, has_side_effects=True),
-    )(*shards)
+    )(*shards, *sent)
 
 
 def placement(route_line, expert_count, capacity):
@@ -268,20 +307,15 @@
         )
         return got.reshape(expert_count * capacity, cols)
 
-    send = jnp.concatenate(
-        [
-            mm(place, rows).astype(BF16).reshape(expert_count, capacity, width)
-            for rows in (tokens[0], scaled_grad)
-        ],
-        axis=1,
+    sent = [
+        mm(place, rows).astype(BF16).reshape(expert_count, capacity, width)
+        for rows in (tokens[0], scaled_grad)
+    ]
+    gate_matrix, up_matrix, down_matrix, routed, routed_grad = gather_weights(
+        dp_count, expert_count, (w_gate[0], w_up[0], w_down[0]), sent
     )
-    arrived = lax.all_to_all(send, "expert", split_axis=0, concat_axis=0, tiled=True)
-    routed = arrived[:, :capacity].reshape(expert_count * capacity, width)
-    routed_grad = arrived[:, capacity:].reshape(expert_count * capacity, width)
-
-    gate_matrix, up_matrix, down_matrix = gather_weights(
-        dp_count, (w_gate[0], w_up[0], w_down[0])
-    )
+    routed = routed.reshape(expert_count * capacity, width)
+    routed_grad = routed_grad.reshape(expert_count * capacity, width)
 
     gate_pre = mm(routed, gate_matrix)
     up_pre = mm(routed, up_matrix)

time: 281 us -> 275 us (0.979)
  starting transfers between devices: 9.84 us -> 4.66 us
  matrix products: 34.1 us -> 37.5 us
    all_to_all x1 -> x0, starting transfers between devices: 5.17 us -> none  [local(): lax.all_to_all(send, 'expert', split_axis=0, concat_axis=0, tiled=True)]
    dot_general x9, matrix products: 34.1 us -> 37.5 us  [mm(): return lax.dot_general(a, b, dims, preferred_element_type=F32)]
  transfers between devices with their start and end apart: 2 -> 1, of which waited for: 0 -> 0; matrix products, arithmetic and copies ran while one was open for 4% -> 5% of each run, Pallas kernels for 81% -> 15%
where the time goes in v4:
time: 275 us; the launch traced here: 274 us
  Pallas kernels  228 us (83%)
  matrix products  37.5 us (14%)
  starting transfers between devices  4.66 us (2%)
    pallas_call x1, Pallas kernels, gather_weights(): pl.pallas_call(functools.partial(gather_kernel, dp_count, expert_count, c...  186 us
    pallas_call x1, Pallas kernels, to_heads(): pl.pallas_call(functools.partial(heads_kernel, expert_count, dp_count), o...  41.8 us
    dot_general x9, matrix products, mm(): return lax.dot_general(a, b, dims, preferred_element_type=F32)  37.5 us
  transfers between devices with their start and end apart: 1, of which 0 were waited for; matrix products, arithmetic and copies ran while one was open for 5% of the time, Pallas kernels for 15%

profile of v4, /device:TPU:0, one launch (start us, length us, event | category | flops | bytes accessed | tf_op | source)
XLA Modules:
  0.0 274.3 jit_solution(13338245505528911510)
XLA Ops:
  0.6 0.0 copy-start
  0.6 0.9 convert_reduce_fusion
  1.6 0.7 fusion.18
  2.2 0.0 copy-done
  2.2 2.2 convolution_convert_fusion.2
  4.5 0.0 copy-done.2
  4.5 2.2 convolution_convert_fusion.1
  6.7 186.4 %shard_map.94 = (bf16[3584,1024]{1,0:T(8,128)(2,1)}, bf16[3584,1024]{1,0:T(8,128)(2,1)}, bf16[1024,3584]{1,0:T(8,128)(2,1)}, bf16[4,80,3584]{2,1,0:T(8,128)(2,1)}, bf16[4,80,3584]{2,1,0:T(8,128)(2,1)}) custom-call(bf16[448,1024]{1,0:T(8,128)(2,1)} %bitcast.49, bf16[448,1024]{1,0:T(8,128)(2,1)} %bitcast.50, bf16[128,3584]{1,0:T(8,128)(2,1)} %bitcast.51, ...), custom_call_target="tpu_custom_call" | custom-call | bytes 550502400 | tf_op jit(solution)/shard_map/pallas_call | solution.py:124
  193.1 0.0 slice-start
  193.1 6.4 %fusion.22 = f32[320,1024]{1,0:T(8,128)S(1)} fusion(bf16[320,3584]{1,0:T(8,128)(2,1)} %bitcast.58, bf16[3584,1024]{1,0:T(8,128)(2,1)} %get-tuple-element.11), kind=kOutput, calls=%fused_computation.36 | convolution fusion | flops 2348810240 | bytes 10944512 | tf_op jit(solution)/shard_map/dot_general | solution.py:158
  199.5 0.0 copy-done.5
  199.6 2.5 fusion.23
  202.1 0.0 copy-start.7
  202.1 0.4 copy-done.4
  202.6 3.6 %fusion.24 = f32[320,1024]{1,0:T(8,128)} fusion(bf16[320,3584]{1,0:T(8,128)(2,1)S(1)} %bitcast.57, bf16[1024,3584]{1,0:T(8,128)(2,1)S(1)} %bitcast.56), kind=kOutput, calls=%fused_computation.38 | convolution fusion | flops 2348810240 | bytes 10944512 | tf_op jit(solution)/shard_map/dot_general | solution.py:158
  206.2 4.1 %convolution_convert_fusion = bf16[320,3584]{1,0:T(8,128)(2,1)} fusion(bf16[1024,3584]{1,0:T(8,128)(2,1)S(1)} %bitcast.56, f32[320,1024]{1,0:T(8,128)S(1)} %fusion.23, f32[320,1024]{1,0:T(8,128)S(1)} %fusion.22), kind=kOutput, calls=%fused_computation.2 | convolution fusion | flops 2351923200 | bytes 12255232 | tf_op jit(solution)/shard_map/dot_general | solution.py:158
  210.3 4.7 %all-to-all-start = ((bf16[4,80,3584]{2,1,0:T(8,128)(2,1)}), bf16[4,80,3584]{2,1,0:T(8,128)(2,1)}, u32[]{:S(2)}, u32[]{:S(2)}) async-start(bf16[4,80,3584]{2,1,0:T(8,128)(2,1)} %bitcast.48), calls=%async_computation | async-start | bytes 4587520 | tf_op jit(solution)/shard_map/all_to_all | solution.py:304
  215.0 0.1 compare_convert_fusion.place
  215.1 6.8 %fusion.9 = f32[320,3584]{1,0:T(8,128)S(1)} fusion(bf16[3584,1024]{1,0:T(8,128)(2,1)} %get-tuple-element.11, f32[320,1024]{1,0:T(8,128)S(1)} %fusion.22, f32[320,1024]{1,0:T(8,128)} %fusion.24, f32[320,1024]{1,0:T(8,128)} %copy-done.7), kind=kOutput, calls=%fused_computation.19 | convolution fusion | flops 2352087040 | bytes 15859712 | tf_op jit(solution)/shard_map/dot_general | solution.py:158
  221.9 5.7 %fusion = bf16[320,3584]{1,0:T(8,128)(2,1)S(1)} fusion(f32[320,3584]{1,0:T(8,128)S(1)} %fusion.9, bf16[3584,1024]{1,0:T(8,128)(2,1)} %get-tuple-element.12, f32[320,1024]{1,0:T(8,128)S(1)} %copy-done.6, f32[320,1024]{1,0:T(8,128)S(1)} %fusion.22), kind=kOutput, calls=%fused_computation.1 | convolution fusion | flops 2353070080 | bytes 16842752 | tf_op jit(solution)/shard_map/dot_general | solution.py:158
  227.6 41.8 %shard_map.95 = bf16[448,1024]{1,0:T(8,128)(2,1)S(1)} custom-call(bf16[4,80,3584]{2,1,0:T(8,128)(2,1)S(1)} %bitcast.45, bf16[4,80,128]{2,1,0:T(8,128)(2,1)S(1)} %compare_convert_fusion.place), custom_call_target="tpu_custom_call" | custom-call | flops 293601280 | bytes 68812800 | tf_op jit(solution)/shard_map/pallas_call | solution.py:264
  269.4 0.0 all-to-all-done
  269.4 3.9 %fusion.2 = (f32[128]{0:T(128)}, bf16[1,128,3584]{2,1,0:T(8,128)(2,1)}) fusion(bf16[1,128,3584]{2,1,0:T(8,128)(2,1)S(1)} %copy-done.1, f32[128]{0:T(128)S(1)} %bitcast.53, bf16[320,3584]{1,0:T(8,128)(2,1)} %bitcast.14, s32[128]{0:T(128)S(1)} %fusion.18), kind=kOutput, calls=%fused_computation.8 | convolution fusion | flops 295935872 | bytes 4130304 | tf_op jit(solution)/shard_map/dot_general | solution.py:158
  273.4 0.9 copy.11
  (15 shorter events, 0.0 us)
Async XLA Ops:
  0.6 1.6 copy-start
  2.2 2.2 copy-start.1
  2.2 2.2 copy-start.2
  193.1 6.5 %copy-start.3 = (bf16[3584,1024]{1,0:T(8,128)(2,1)S(1)}, bf16[3584,1024]{1,0:T(8,128)(2,1)}, u32[]{:S(2)}) copy-start(bf16[3584,1024]{1,0:T(8,128)(2,1)} %get-tuple-element.12) | copy-start | bytes 22020100
  193.1 6.5 %copy-start.5 = (bf16[4,80,3584]{2,1,0:T(8,128)(2,1)S(1)}, bf16[4,80,3584]{2,1,0:T(8,128)(2,1)}, u32[]{:S(2)}) copy-start(bf16[4,80,3584]{2,1,0:T(8,128)(2,1)} %get-tuple-element.10) | copy-start | bytes 6881284
  193.1 9.0 %slice-start = ((s8[7340032]{0:T(1024)(128)(4,1)}), s8[4194304]{0:T(1024)(128)(4,1)S(1)}, s32[]{:S(2)}) async-start(s8[7340032]{0:T(1024)(128)(4,1)} %bitcast.55), calls=%async_computation.1 | async-start | bytes 8388608
  199.6 2.6 slice-start.1
  199.6 3.0 %copy-start.4 = (bf16[4,80,3584]{2,1,0:T(8,128)(2,1)S(1)}, bf16[4,80,3584]{2,1,0:T(8,128)(2,1)}, u32[]{:S(2)}) copy-start(bf16[4,80,3584]{2,1,0:T(8,128)(2,1)} %get-tuple-element.14) | copy-start | bytes 6881284
  202.1 4.1 %copy-start.7 = (f32[320,1024]{1,0:T(8,128)}, f32[320,1024]{1,0:T(8,128)S(1)}, u32[]{:S(2)}) copy-start(f32[320,1024]{1,0:T(8,128)S(1)} %fusion.23) | copy-start | bytes 3932164
  210.3 59.1 %all-to-all-start = ((bf16[4,80,3584]{2,1,0:T(8,128)(2,1)}), bf16[4,80,3584]{2,1,0:T(8,128)(2,1)}, u32[]{:S(2)}, u32[]{:S(2)}) async-start(bf16[4,80,3584]{2,1,0:T(8,128)(2,1)} %bitcast.48), calls=%async_computation | async-start | bytes 4587520 | tf_op jit(solution)/shard_map/all_to_all | solution.py:304
  215.1 6.8 %copy-start.6 = (f32[320,1024]{1,0:T(8,128)S(1)}, f32[320,1024]{1,0:T(8,128)}, u32[]{:S(2)}) copy-start(f32[320,1024]{1,0:T(8,128)} %fusion.24) | copy-start | bytes 3932164
